TPU v7x, 32 devices: a whole 2x2x4 slice. The times are simulated.
32 devices in a mesh: tm: 4 (over y, core), slab: 8 (over z, x).
Axes of the slice: x: 2, y: 2, z: 4, core: 2. Of those that a mesh axis runs over, the one named last changes fastest.
Arguments:
- solutions: float32 [4, 96, 8192], P('tm', None, 'slab'), may hold values from -6 to 6
- eigvecs: float32 [4, 2, 192, 3, 8192], P('tm', None, None, None, 'slab'), may hold values from -0.02734375 to 0.02734375
- sink_noise: int32 [192, 4, 4], P(None, 'tm'), may hold values from 0 to 3
- eig_block: int32 [192], replicated, may hold values from 0 to 7
Outputs:
- projected: float32 [192, 4, 2, 16], P('slab', 'tm')
- sink_line: float32 [2, 8, 4], replicated
All inputs are finite; a program needn't handle non-finite values.
Results may differ from a plain program's by a relative error of at most 0.000092.
Values sent between devices are 32-bit elements; how exact they have to be, the bound alone decides.
No kernel may reach another device: no remote copies, remote signals or barrier semaphores. Data moves between devices by JAX's collectives and lax.ppermute only.
A program may use at most 128 MiB of HBM per device.

v0:
```python
import math

import jax
import jax.numpy as jnp
from jax import lax
from jax.sharding import PartitionSpec as P

NSPIN = 4
NCOLOR = 3
NEIG = 192
NBLOCK = 8


def project(vectors, columns):
    product = jnp.einsum("akcs,bjcs->abkj", vectors, columns, precision=lax.Precision.HIGHEST)
    return jnp.stack((product[0, 0] + product[1, 1], product[0, 1] - product[1, 0]), axis=1)


def line_part(parts, sink_noise, eig_block):
    real_part = parts[:, :, 0]
    imag_part = parts[:, :, 1]
    zreal = ((sink_noise == 0).astype(jnp.float32) - (sink_noise == 2).astype(jnp.float32))[
        ..., None
    ]
    zimag = ((sink_noise == 1).astype(jnp.float32) - (sink_noise == 3).astype(jnp.float32))[
        ..., None
    ]
    line_real = jnp.sum(zreal * real_part + zimag * imag_part, axis=(1, 2))
    line_imag = jnp.sum(zreal * imag_part - zimag * real_part, axis=(1, 2))
    onehot = (eig_block[:, None] == jnp.arange(NBLOCK, dtype=jnp.int32)[None, :]).astype(
        jnp.float32
    )
    return jnp.stack(
        (
            jnp.dot(onehot.T, line_real, precision=lax.Precision.HIGHEST),
            jnp.dot(onehot.T, line_imag, precision=lax.Precision.HIGHEST),
        )
    )


def body(solutions, eigvecs, sink_noise, eig_block):
    slab_count = lax.axis_size("slab")
    per_device = NEIG // slab_count
    spin_pairs = NSPIN * NSPIN
    outgoing = solutions.reshape(2, spin_pairs, NCOLOR, -1, slab_count)
    vectors = eigvecs.reshape(2, NEIG, NCOLOR, -1)
    received = lax.all_to_all(outgoing, "slab", split_axis=4, concat_axis=4, tiled=True)
    partial_sums = project(vectors, received.reshape(2, received.shape[1], NCOLOR, -1))
    slab_index = lax.axis_index("slab")
    own_rows = lax.psum_scatter(partial_sums, "slab", scatter_dimension=0, tiled=True)
    noise_rows = lax.dynamic_slice_in_dim(sink_noise, slab_index * per_device, per_device, 0)
    block_rows = lax.dynamic_slice_in_dim(eig_block, slab_index * per_device, per_device, 0)
    local_line = line_part(own_rows.reshape(per_device, 1, 2, NSPIN, NSPIN), noise_rows, block_rows)
    sink_line = lax.psum(local_line, ("tm", "slab"))
    factor = 1.0 / math.sqrt(lax.axis_size("tm") * NEIG * NSPIN / NBLOCK)
    projected = own_rows.reshape(per_device, 1, 2, spin_pairs)
    return (projected, sink_line * factor)


def solution(mesh):
    in_specs = (P("tm", None, "slab"), P("tm", None, None, None, "slab"), P(None, "tm", None), P())
    out_specs = (P("slab", "tm", None, None), P())
    return jax.shard_map(body, mesh=mesh, in_specs=in_specs, out_specs=out_specs, check_vma=False)
```

profile of v0, /device:TPU:0, one launch (start us, length us, event | category | flops | bytes accessed | tf_op | source)
XLA Modules:
  0.0 117.3 jit_solution(14614706557704698208)
XLA Ops:
  0.6 5.9 %reshape.118 = f32[2,16,3,128,8]{4,3,2,1,0:T(8,128)} reshape(f32[1,96,1024]{2,1,0:T(8,128)} %param.4) | data formatting | bytes 786432 | tf_op jit(solution)/shard_map/reshape | solution.py:45
  6.5 0.0 copy-start.2
  6.5 0.0 copy-start.1
  6.5 0.0 copy-start
  6.5 5.2 %copy.13 = f32[2,16,3,128,8]{3,1,2,0,4:T(8,128)} copy(f32[2,16,3,128,8]{4,3,2,1,0:T(8,128)} %reshape.118) | data formatting | bytes 786432 | tf_op jit(solution)/shard_map/reshape | solution.py:45
  11.7 7.3 %all-to-all-start = ((f32[2,16,3,128,8]{3,1,2,0,4:T(8,128)}), f32[2,16,3,128,8]{3,1,2,0,4:T(8,128)S(1)}, u32[]{:S(2)}, u32[]{:S(2)}) async-start(f32[2,16,3,128,8]{3,1,2,0,4:T(8,128)} %copy.13), calls=%async_computation | async-start | bytes 786432 | tf_op jit(solution)/shard_map/all_to_all | solution.py:47
  18.9 0.0 copy-done.2
  18.9 0.6 dynamic-slice
  20.2 0.0 copy-done.1
  20.2 0.1 dynamic_slice.6
  20.3 0.0 copy-done
  20.3 0.1 subtract_bitcast_fusion.1
  20.3 10.3 %all-to-all-done = f32[2,16,3,128,8]{3,1,2,0,4:T(8,128)S(1)} async-done(((f32[2,16,3,128,8]{3,1,2,0,4:T(8,128)}), f32[2,16,3,128,8]{3,1,2,0,4:T(8,128)S(1)}, u32[]{:S(2)}, u32[]{:S(2)}) %all-to-all-start) | async-done | bytes 393248 | tf_op jit(solution)/shard_map/all_to_all | solution.py:47
  30.6 1.1 copy.14
  31.8 11.7 %fusion.3 = f32[2,2,192,16]{2,3,0,1:T(8,128)S(1)} fusion(f32[1,2,192,3,1024]{4,2,3,1,0:T(8,128)} %param.5, f32[2,16,3,128,8]{1,4,3,2,0:T(8,128)S(1)} %copy.14), kind=kOutput, calls=%fused_computation.3 | convolution fusion | flops 452984832 | bytes 5160960 | tf_op jit(solution)/shard_map/akcs,bjcs->abkj/dot_general | solution.py:15
  43.5 35.2 %all-reduce = f32[192,2,16]{0,2,1:T(8,128)S(1)} all-reduce(f32[192,2,16]{0,2,1:T(8,128)S(1)} %pad_maximum_fusion), channel_id=2, replica_groups=mesh['tm'=4,'slab'=8] {'slab'}, use_global_device_ids=true, to_apply=%region_0.0.clone | all-reduce | flops 6144 | bytes 49152
  78.7 0.7 fusion.15
  79.4 0.1 constant_dynamic-slice_fusion
  79.5 0.2 convolution_bitcast_fusion
  79.7 0.2 convolution_bitcast_fusion.1
  79.9 36.9 %psum.7 = f32[2,8,4]{1,2,0:T(4,128)S(1)} all-reduce(f32[2,8,4]{1,2,0:T(4,128)S(1)} %pad_maximum_fusion.1), channel_id=1, replica_groups=mesh['tm'=4,'slab'=8] {'tm','slab'}, use_global_device_ids=true, to_apply=%region_3.0 | all-reduce | flops 64 | bytes 512 | tf_op jit(solution)/shard_map/psum | solution.py:54
  116.7 0.6 broadcast_multiply_fusion
  (5 shorter events, 0.0 us)
Async XLA Ops:
  6.5 12.4 %copy-start.2 = (u32[32]{0:T(128)S(1)}, u32[32]{0:T(128)}, u32[]{:S(2)}) copy-start(u32[32]{0:T(128)} %constant.26) | copy-start | bytes 388
  6.5 13.7 %copy-start.1 = (s32[192]{0:T(256)S(1)}, s32[192]{0:T(256)}, u32[]{:S(2)}) copy-start(s32[192]{0:T(256)} %param.7) | copy-start | bytes 2308
  6.5 13.8 %copy-start = (s32[192,1,4]{0,2,1:T(4,128)S(1)}, s32[192,1,4]{0,2,1:T(4,128)}, u32[]{:S(2)}) copy-start(s32[192,1,4]{0,2,1:T(4,128)} %param.6) | copy-start | bytes 9220
  11.7 18.9 %all-to-all-start = ((f32[2,16,3,128,8]{3,1,2,0,4:T(8,128)}), f32[2,16,3,128,8]{3,1,2,0,4:T(8,128)S(1)}, u32[]{:S(2)}, u32[]{:S(2)}) async-start(f32[2,16,3,128,8]{3,1,2,0,4:T(8,128)} %copy.13), calls=%async_computation | async-start | bytes 786432 | tf_op jit(solution)/shard_map/all_to_all | solution.py:47
where the time goes:
time: 118 us; the launch traced here: 117 us
  blocking collectives  72.1 us (61%)
  local copies, waits for them, and re-layouts  13.6 us (12%)
  matrix products  12.1 us (10%)
  waiting for transfers between devices  10.3 us (9%)
  starting transfers between devices  7.25 us (6%)
  between operations  1.33 us (1%)
    psum x1, blocking collectives, body(): sink_line = lax.psum(local_line, ('tm', 'slab'))  36.9 us
    unnamed x1, blocking collectives  35.2 us
    dot_general x1, matrix products, project(): jnp.einsum('akcs,bjcs->abkj', vectors, columns, precision=lax.Precision.H...  11.7 us
    reshape x2, local copies, waits for them, and re-layouts, body(): outgoing = solutions.reshape(2, spin_pairs, NCOLOR, -1, slab_count)  11 us
    all_to_all x1, waiting for transfers between devices, body(): lax.all_to_all(outgoing, 'slab', split_axis=4, concat_axis=4, tiled=True)  10.3 us
    all_to_all x1, starting transfers between devices, body(): lax.all_to_all(outgoing, 'slab', split_axis=4, concat_axis=4, tiled=True)  7.25 us
  transfers between devices with their start and end apart: 1, of which 1 were waited for; matrix products, arithmetic and copies ran while one was open for 1% of the time, Pallas kernels for 0%

commit v1 on v0

v1 whole, which is shorter than its diff:
```python
import functools
import math

import jax
import jax.numpy as jnp
from jax import lax
from jax.experimental import pallas as pl
from jax.experimental.pallas import tpu as pltpu
from jax.sharding import PartitionSpec as P

NSPIN = 4
NCOLOR = 3
NEIG = 192
NBLOCK = 8
PAIRS = NSPIN * NSPIN
COLS = 2 * PAIRS
GROUPS = 128 // COLS
LINE_LANE = 96

VMEM = pl.BlockSpec(memory_space=pltpu.VMEM)
SMEM = pl.BlockSpec(memory_space=pltpu.SMEM)


def split(value):
    high = value.astype(jnp.bfloat16)
    low = (value - high.astype(jnp.float32)).astype(jnp.bfloat16)
    return high, low


def pack_kernel(count, sol_ref, out_ref, tiles, turned):
    width = sol_ref.shape[1] // GROUPS
    rows = width // count
    for i in range(tiles.shape[0]):
        tiles[i] = sol_ref[:, pl.ds(128 * i, 128)]
    per_group = width // 128
    for color in range(NCOLOR):
        for i in range(per_group):
            stacked = jnp.concatenate(
                [tiles[g * per_group + i, pl.ds(color, COLS, stride=NCOLOR), :] for g in range(GROUPS)], axis=0
            )
            turned[pl.ds(128 * i, 128), :] = stacked.T
        for r in range(count):
            out_ref[r, pl.ds(color * rows, rows), :] = turned[pl.ds(r, rows, stride=count), :]


def project_kernel(count, field_ref, vec_ref, noise_ref, block_ref, out_ref, weights):
    width = vec_ref.shape[3] // GROUPS
    rows = width // count
    per = NEIG // count
    for color in range(NCOLOR):
        for s in range(count):
            weights[pl.ds(color * width + s, rows, stride=count), :] = field_ref[s, pl.ds(color * rows, rows), :]
    high, low = split(weights[...])
    both = jnp.concatenate([high, low], axis=1)
    lane = lax.broadcasted_iota(jnp.int32, (NEIG, 128), 1)
    sums = []
    for part in range(2):
        total = jnp.zeros((NEIG, 128), jnp.float32)
        for g in range(GROUPS):
            vec = jnp.concatenate([vec_ref[part, color, :, pl.ds(g * width, width)] for color in range(NCOLOR)], axis=1)
            vec_high, vec_low = split(vec)
            first = jnp.dot(vec_high, both, preferred_element_type=jnp.float32)
            second = jnp.dot(vec_low, high, preferred_element_type=jnp.float32)
            value = first[:, :128] + (first[:, 128:] + second)
            total = jnp.where(lane // COLS == g, value, total)
        shift = 64
        while shift >= COLS:
            total = total + pltpu.roll(total, shift, axis=1)
            shift //= 2
        sums.append(total)
    swapped = pltpu.roll(sums[1], PAIRS, axis=1)
    product = sums[0] + jnp.where(lane % COLS < PAIRS, swapped, -swapped)
    turned = product.T[:COLS]
    real, imag = turned[:PAIRS], turned[PAIRS:]
    noise = jnp.concatenate(
        [jnp.broadcast_to(noise_ref[pl.ds(spin, 1), :], (NSPIN, NEIG)) for spin in range(NSPIN)], axis=0
    )
    zreal = (noise == 0).astype(jnp.float32) - (noise == 2).astype(jnp.float32)
    zimag = (noise == 1).astype(jnp.float32) - (noise == 3).astype(jnp.float32)
    line = jnp.concatenate([zreal * real + zimag * imag, zreal * imag - zimag * real], axis=0)
    blocks = lax.broadcasted_iota(jnp.int32, (NBLOCK, NEIG), 0)
    onehot = (blocks == block_ref[...]).astype(jnp.bfloat16)
    line_high, line_low = split(line)
    dims = (((1,), (1,)), ((), ()))
    line_sum = lax.dot_general(onehot, line_high, dims, preferred_element_type=jnp.float32)
    line_sum += lax.dot_general(onehot, line_low, dims, preferred_element_type=jnp.float32)
    packed = [None] * count
    for j in range(count):
        pieces = [turned[8 * i : 8 * i + 8, per * j : per * (j + 1)] for i in range(COLS // 8)]
        used = per * len(pieces)
        if used < LINE_LANE:
            pieces.append(jnp.zeros((8, LINE_LANE - used), jnp.float32))
        packed[j] = jnp.concatenate(pieces + [line_sum], axis=1)
    for i in range(out_ref.shape[0]):
        for j in range(count):
            out_ref[i, j] = packed[j]


def finish_kernel(count, factor, index_ref, parts_ref, rows_ref, line_ref):
    per = NEIG // count
    own = jnp.sum(parts_ref[index_ref[0]], axis=0)
    for i in range(COLS // 8):
        rows_ref[pl.ds(8 * i, 8), :] = own[:, per * i : per * (i + 1)]
    whole = jnp.sum(jnp.sum(parts_ref[...], axis=1), axis=0)
    turned = whole.T[LINE_LANE:]
    for part in range(2):
        first = PAIRS * part
        line_ref[part] = factor * sum(turned[first + NSPIN * s : first + NSPIN * (s + 1)] for s in range(NSPIN))


def body(solutions, eigvecs, sink_noise, eig_block):
    count = lax.axis_size("slab")
    times = lax.axis_size("tm")
    sites = solutions.shape[-1]
    rows = NCOLOR * sites // GROUPS // count
    per = NEIG // count
    f32 = jnp.float32
    chunks = pl.pallas_call(
        functools.partial(pack_kernel, count),
        out_shape=jax.ShapeDtypeStruct((count, rows, 128), f32),
        in_specs=[VMEM],
        out_specs=VMEM,
        scratch_shapes=[pltpu.VMEM((sites // 128, NCOLOR * COLS, 128), f32), pltpu.VMEM((sites // GROUPS, 128), f32)],
        compiler_params=pltpu.CompilerParams(vmem_limit_bytes=8 * 1024 * 1024),
        name="pack",
    )(solutions.reshape(solutions.shape[1:]))
    received = lax.all_to_all(chunks, "slab", split_axis=0, concat_axis=0, tiled=True)
    vectors = jnp.transpose(eigvecs.reshape(eigvecs.shape[1:]), (0, 2, 1, 3))
    parts = pl.pallas_call(
        functools.partial(project_kernel, count),
        out_shape=jax.ShapeDtypeStruct((times, count, 8, 128), f32),
        in_specs=[VMEM] * 4,
        out_specs=VMEM,
        scratch_shapes=[pltpu.VMEM((NCOLOR * sites // GROUPS, 128), f32)],
        compiler_params=pltpu.CompilerParams(vmem_limit_bytes=32 * 1024 * 1024),
        name="project",
    )(received, vectors, jnp.transpose(sink_noise.reshape(NEIG, NSPIN)), eig_block.reshape(1, NEIG))
    parts = lax.all_to_all(parts.reshape(times * count, 8, 128), ("tm", "slab"), split_axis=0, concat_axis=0, tiled=True)
    factor = 1.0 / math.sqrt(times * NEIG * NSPIN / NBLOCK)
    own_rows, line = pl.pallas_call(
        functools.partial(finish_kernel, count, factor),
        out_shape=(jax.ShapeDtypeStruct((COLS, per), f32), jax.ShapeDtypeStruct((2, NSPIN, NBLOCK), f32)),
        in_specs=[SMEM, VMEM],
        out_specs=(VMEM, VMEM),
        compiler_params=pltpu.CompilerParams(vmem_limit_bytes=8 * 1024 * 1024),
        name="finish",
    )(lax.axis_index("tm").reshape(1), parts.reshape(times, count, 8, 128))
    projected = jnp.transpose(own_rows).reshape(per, 1, 2, PAIRS)
    return projected, jnp.transpose(line, (0, 2, 1))


def solution(mesh):
    in_specs = (P("tm", None, "slab"), P("tm", None, None, None, "slab"), P(None, "tm", None), P())
    out_specs = (P("slab", "tm", None, None), P())
    return jax.shard_map(body, mesh=mesh, in_specs=in_specs, out_specs=out_specs, check_vma=False)
```

time: 118 us -> 39.3 us (0.33)
  blocking collectives: 72.1 us -> 19.1 us
  matrix products: 12.1 us -> 0 us
  local copies, waits for them, and re-layouts: 13.6 us -> 4.69 us
  starting transfers between devices: 7.25 us -> 3.26 us
  Pallas kernels: 0 us -> 3.5 us
  waiting for transfers between devices: 10.3 us -> 7.73 us
    psum x1 -> x0, blocking collectives: 36.9 us -> none  [body(): sink_line = lax.psum(local_line, ('tm', 'slab'))]
    unnamed x1 -> x0, blocking collectives: 35.2 us -> none
    all_to_all x0 -> x1, blocking collectives: none -> 19.1 us  [body(): lax.all_to_all(chunks, 'slab', split_axis=0, concat_axis=0, tiled=True)]
    dot_general x3 -> x0, matrix products: 12.1 us -> none  [the longest x1 11.7 us: project(): jnp.einsum('akcs,bjcs->abkj', vectors, columns, precision=lax.Precision.H...]
    reshape x3 -> x0, local copies, waits for them, and re-layouts: 11.7 us -> none  [the longest x2 11 us: body(): outgoing = solutions.reshape(2, spin_pairs, NCOLOR, -1, slab_count)]
    unnamed x8, local copies, waits for them, and re-layouts: 0.67 us -> 4.69 us
    all_to_all x1, starting transfers between devices: 7.25 us -> 3.26 us  [body(): lax.all_to_all(parts.reshape(times * count, 8, 128), ('tm', 'slab'), spli...]
    pallas_call x0 -> x3, Pallas kernels: none -> 3.5 us  [the longest x1 2.56 us: body(): pl.pallas_call(functools.partial(project_kernel, count), out_shape=jax.Sh...]
  transfers between devices with their start and end apart: 1 -> 1, of which waited for: 1 -> 1; matrix products, arithmetic and copies ran while one was open for 1% -> 0% of each run, Pallas kernels for 0% -> 0%
where the time goes in v1:
time: 39.3 us; the launch traced here: 39 us
  blocking collectives  19.1 us (49%)
  waiting for transfers between devices  7.73 us (20%)
  local copies, waits for them, and re-layouts  4.69 us (12%)
  Pallas kernels  3.5 us (9%)
  starting transfers between devices  3.26 us (8%)
  between operations  0.66 us (2%)
    all_to_all x1, blocking collectives, body(): lax.all_to_all(chunks, 'slab', split_axis=0, concat_axis=0, tiled=True)  19.1 us
    all_to_all x1, waiting for transfers between devices, body(): lax.all_to_all(parts.reshape(times * count, 8, 128), ('tm', 'slab'), spli...  7.73 us
    unnamed x8, local copies, waits for them, and re-layouts  4.69 us
    all_to_all x1, starting transfers between devices, body(): lax.all_to_all(parts.reshape(times * count, 8, 128), ('tm', 'slab'), spli...  3.26 us
    pallas_call x1, Pallas kernels, body(): pl.pallas_call(functools.partial(project_kernel, count), out_shape=jax.Sh...  2.56 us
  transfers between devices with their start and end apart: 1, of which 1 were waited for; matrix products, arithmetic and copies ran while one was open for 0% of the time, Pallas kernels for 0%

profile of v1, /device:TPU:0, one launch (start us, length us, event | category | flops | bytes accessed | tf_op | source)
XLA Modules:
  0.0 39.0 jit_solution(17971775674709918278)
XLA Ops:
  0.6 0.0 copy-start.1
  0.6 1.0 %copy-done.1 = f32[1,96,1024]{2,1,0:T(8,128)S(1)} copy-done((f32[1,96,1024]{2,1,0:T(8,128)S(1)}, f32[1,96,1024]{2,1,0:T(8,128)}, u32[]{:S(2)}) %copy-start.1) | copy-done | bytes 393240
  1.6 0.2 pack.1
  1.8 19.1 %all_to_all.10.field_ref = f32[8,96,128]{2,1,0:T(8,128)S(1)} all-to-all(f32[8,96,128]{2,1,0:T(8,128)S(1)} %pack.1), channel_id=1, replica_groups=mesh['tm'=4,'slab'=8] {'slab'}, dimensions={0} | all-to-all | bytes 786432 | tf_op jit(solution)/shard_map/all_to_all | solution.py:127
  21.0 0.0 copy-start
  21.0 2.3 %copy-done = f32[1,2,192,3,1024]{4,2,3,1,0:T(8,128)S(1)} copy-done((f32[1,2,192,3,1024]{4,2,3,1,0:T(8,128)S(1)}, f32[1,2,192,3,1024]{4,2,3,1,0:T(8,128)}, u32[]{:S(2)}) %copy-start) | copy-done | bytes 4718616
  23.3 0.0 copy-start.2
  23.3 0.7 %copy-done.2 = s32[192,1,4]{0,2,1:T(4,128)S(1)} copy-done((s32[192,1,4]{0,2,1:T(4,128)S(1)}, s32[192,1,4]{0,2,1:T(4,128)}, u32[]{:S(2)}) %copy-start.2) | copy-done | bytes 3096
  24.0 0.0 copy-start.3
  24.0 0.7 %copy-done.3 = s32[192]{0:T(256)S(1)} copy-done((s32[192]{0:T(256)S(1)}, s32[192]{0:T(256)}, u32[]{:S(2)}) %copy-start.3) | copy-done | bytes 792
  24.7 2.6 %project.1 = f32[4,8,8,128]{3,2,1,0:T(8,128)} custom-call(f32[8,96,128]{2,1,0:T(8,128)S(1)} %all_to_all.10.field_ref, f32[2,3,192,1024]{3,2,1,0:T(8,128)S(1)} %bitcast.15, s32[4,192]{1,0:T(4,128)S(1)} %bitcast.18, s32[1,192]{1,0:T(1,128)S(1)} %bitcast.19), custom_call_target="tpu_custom_call" | custom-call | tf_op jit(solution)/shard_map/project/pallas_call | solution.py:129
  27.2 3.3 %all-to-all-start.1 = ((f32[32,8,128]{2,1,0:T(8,128)}), f32[32,8,128]{2,1,0:T(8,128)S(1)}, u32[]{:S(2)}, u32[]{:S(2)}) async-start(f32[32,8,128]{2,1,0:T(8,128)} %bitcast.7), calls=%async_computation.1 | async-start | bytes 262144 | tf_op jit(solution)/shard_map/all_to_all | solution.py:138
  30.5 7.7 %all-to-all-done.1 = f32[32,8,128]{2,1,0:T(8,128)S(1)} async-done(((f32[32,8,128]{2,1,0:T(8,128)}), f32[32,8,128]{2,1,0:T(8,128)S(1)}, u32[]{:S(2)}, u32[]{:S(2)}) %all-to-all-start.1) | async-done | bytes 131104 | tf_op jit(solution)/shard_map/all_to_all | solution.py:138
  38.3 0.7 %finish.1 = (f32[32,24]{1,0:T(8,128)}, f32[2,4,8]{2,1,0:T(4,128)}) custom-call(s32[1]{0:T(128)} %bitcast.index_ref, f32[4,8,8,128]{3,2,1,0:T(8,128)S(1)} %bitcast.16), custom_call_target="tpu_custom_call" | custom-call | tf_op jit(solution)/shard_map/finish/pallas_call | solution.py:140
Async XLA Ops:
  0.6 1.0 %copy-start.1 = (f32[1,96,1024]{2,1,0:T(8,128)S(1)}, f32[1,96,1024]{2,1,0:T(8,128)}, u32[]{:S(2)}) copy-start(f32[1,96,1024]{2,1,0:T(8,128)} %param.4) | copy-start | bytes 1179652
  21.0 2.3 %copy-start = (f32[1,2,192,3,1024]{4,2,3,1,0:T(8,128)S(1)}, f32[1,2,192,3,1024]{4,2,3,1,0:T(8,128)}, u32[]{:S(2)}) copy-start(f32[1,2,192,3,1024]{4,2,3,1,0:T(8,128)} %param.5) | copy-start | bytes 14155780
  23.3 0.7 %copy-start.2 = (s32[192,1,4]{0,2,1:T(4,128)S(1)}, s32[192,1,4]{0,2,1:T(4,128)}, u32[]{:S(2)}) copy-start(s32[192,1,4]{0,2,1:T(4,128)} %param.6) | copy-start | bytes 9220
  24.0 0.7 %copy-start.3 = (s32[192]{0:T(256)S(1)}, s32[192]{0:T(256)}, u32[]{:S(2)}) copy-start(s32[192]{0:T(256)} %param.7) | copy-start | bytes 2308
  27.2 11.0 %all-to-all-start.1 = ((f32[32,8,128]{2,1,0:T(8,128)}), f32[32,8,128]{2,1,0:T(8,128)S(1)}, u32[]{:S(2)}, u32[]{:S(2)}) async-start(f32[32,8,128]{2,1,0:T(8,128)} %bitcast.7), calls=%async_computation.1 | async-start | bytes 262144 | tf_op jit(solution)/shard_map/all_to_all | solution.py:138

commit v2 on v1

--- a/solution.py
+++ b/solution.py
@@ -17,6 +17,8 @@
 GROUPS = 128 // COLS
 LINE_LANE = 96
 
+ORDER = (4, 6, 5, 7, 1, 3, 2)
+
 VMEM = pl.BlockSpec(memory_space=pltpu.VMEM)
 SMEM = pl.BlockSpec(memory_space=pltpu.SMEM)
 
@@ -27,42 +29,58 @@
     return high, low
 
 
-def pack_kernel(count, sol_ref, out_ref, tiles, turned):
+def pack_kernel(partners, index_ref, sol_ref, *refs):
+    out_refs, (tiles, turned) = refs[: len(partners)], refs[len(partners) :]
+    count = len(partners)
     width = sol_ref.shape[1] // GROUPS
     rows = width // count
+    per_group = width // 128
     for i in range(tiles.shape[0]):
         tiles[i] = sol_ref[:, pl.ds(128 * i, 128)]
-    per_group = width // 128
     for color in range(NCOLOR):
         for i in range(per_group):
             stacked = jnp.concatenate(
                 [tiles[g * per_group + i, pl.ds(color, COLS, stride=NCOLOR), :] for g in range(GROUPS)], axis=0
             )
             turned[pl.ds(128 * i, 128), :] = stacked.T
-        for r in range(count):
-            out_ref[r, pl.ds(color * rows, rows), :] = turned[pl.ds(r, rows, stride=count), :]
+        for partner, out_ref in zip(partners, out_refs):
+            r = jnp.bitwise_xor(index_ref[0], partner)
+            out_ref[pl.ds(color * rows, rows), :] = turned[pl.ds(r, rows, stride=count), :]
 
 
-def project_kernel(count, field_ref, vec_ref, noise_ref, block_ref, out_ref, weights):
+def split_kernel(vec_ref, high_ref, low_ref):
     width = vec_ref.shape[3] // GROUPS
+    for part in range(2):
+        for g in range(GROUPS):
+            rows = pl.ds((part * GROUPS + g) * NEIG, NEIG)
+            for color in range(NCOLOR):
+                lanes = pl.ds(color * width, width)
+                high, low = split(vec_ref[part, color, :, pl.ds(g * width, width)])
+                high_ref[rows, lanes] = high
+                low_ref[rows, lanes] = low
+
+
+def project_kernel(partners, index_ref, *refs):
+    count = len(partners)
+    field_refs = refs[:count]
+    high_ref, low_ref, noise_ref, block_ref, out_ref, weights = refs[count:]
+    width = high_ref.shape[1] // NCOLOR
     rows = width // count
     per = NEIG // count
-    for color in range(NCOLOR):
-        for s in range(count):
-            weights[pl.ds(color * width + s, rows, stride=count), :] = field_ref[s, pl.ds(color * rows, rows), :]
+    for partner, field_ref in zip(partners, field_refs):
+        s = jnp.bitwise_xor(index_ref[0], partner)
+        for color in range(NCOLOR):
+            weights[pl.ds(color * width + s, rows, stride=count), :] = field_ref[pl.ds(color * rows, rows), :]
     high, low = split(weights[...])
-    both = jnp.concatenate([high, low], axis=1)
+    first = jnp.dot(high_ref[...], jnp.concatenate([high, low], axis=1), preferred_element_type=jnp.float32)
+    second = jnp.dot(low_ref[...], high, preferred_element_type=jnp.float32)
+    products = first[:, :128] + (first[:, 128:] + second)
     lane = lax.broadcasted_iota(jnp.int32, (NEIG, 128), 1)
     sums = []
     for part in range(2):
-        total = jnp.zeros((NEIG, 128), jnp.float32)
-        for g in range(GROUPS):
-            vec = jnp.concatenate([vec_ref[part, color, :, pl.ds(g * width, width)] for color in range(NCOLOR)], axis=1)
-            vec_high, vec_low = split(vec)
-            first = jnp.dot(vec_high, both, preferred_element_type=jnp.float32)
-            second = jnp.dot(vec_low, high, preferred_element_type=jnp.float32)
-            value = first[:, :128] + (first[:, 128:] + second)
-            total = jnp.where(lane // COLS == g, value, total)
+        total = products[part * GROUPS * NEIG :][:NEIG]
+        for g in range(1, GROUPS):
+            total = jnp.where(lane // COLS == g, products[(part * GROUPS + g) * NEIG :][:NEIG], total)
         shift = 64
         while shift >= COLS:
             total = total + pltpu.roll(total, shift, axis=1)
@@ -115,26 +133,42 @@
     rows = NCOLOR * sites // GROUPS // count
     per = NEIG // count
     f32 = jnp.float32
+    index = lax.axis_index("slab").reshape(1)
+    far = [p for p in ORDER if p < count]
+    partners = [0] + far + [p for p in range(1, count) if p not in far]
     chunks = pl.pallas_call(
-        functools.partial(pack_kernel, count),
-        out_shape=jax.ShapeDtypeStruct((count, rows, 128), f32),
-        in_specs=[VMEM],
-        out_specs=VMEM,
+        functools.partial(pack_kernel, partners),
+        out_shape=[jax.ShapeDtypeStruct((rows, 128), f32)] * count,
+        in_specs=[SMEM, VMEM],
+        out_specs=[VMEM] * count,
         scratch_shapes=[pltpu.VMEM((sites // 128, NCOLOR * COLS, 128), f32), pltpu.VMEM((sites // GROUPS, 128), f32)],
         compiler_params=pltpu.CompilerParams(vmem_limit_bytes=8 * 1024 * 1024),
         name="pack",
-    )(solutions.reshape(solutions.shape[1:]))
-    received = lax.all_to_all(chunks, "slab", split_axis=0, concat_axis=0, tiled=True)
+    )(index, solutions.reshape(solutions.shape[1:]))
+    received = [
+        lax.ppermute(chunk, "slab", [(i, i ^ partner) for i in range(count)]) if partner else chunk
+        for partner, chunk in zip(partners, chunks)
+    ]
     vectors = jnp.transpose(eigvecs.reshape(eigvecs.shape[1:]), (0, 2, 1, 3))
+    shape = jax.ShapeDtypeStruct((2 * GROUPS * NEIG, NCOLOR * sites // GROUPS), jnp.bfloat16)
+    high, low = pl.pallas_call(
+        split_kernel,
+        out_shape=(shape, shape),
+        in_specs=[VMEM],
+        out_specs=(VMEM, VMEM),
+        compiler_params=pltpu.CompilerParams(vmem_limit_bytes=24 * 1024 * 1024),
+        cost_estimate=pl.CostEstimate(flops=6 * eigvecs.size, bytes_accessed=8 * eigvecs.size, transcendentals=0),
+        name="split",
+    )(vectors)
     parts = pl.pallas_call(
-        functools.partial(project_kernel, count),
+        functools.partial(project_kernel, partners),
         out_shape=jax.ShapeDtypeStruct((times, count, 8, 128), f32),
-        in_specs=[VMEM] * 4,
+        in_specs=[SMEM] + [VMEM] * (count + 4),
         out_specs=VMEM,
         scratch_shapes=[pltpu.VMEM((NCOLOR * sites // GROUPS, 128), f32)],
-        compiler_params=pltpu.CompilerParams(vmem_limit_bytes=32 * 1024 * 1024),
+        compiler_params=pltpu.CompilerParams(vmem_limit_bytes=24 * 1024 * 1024),
         name="project",
-    )(received, vectors, jnp.transpose(sink_noise.reshape(NEIG, NSPIN)), eig_block.reshape(1, NEIG))
+    )(index, *received, high, low, jnp.transpose(sink_noise.reshape(NEIG, NSPIN)), eig_block.reshape(1, NEIG))
     parts = lax.all_to_all(parts.reshape(times * count, 8, 128), ("tm", "slab"), split_axis=0, concat_axis=0, tiled=True)
     factor = 1.0 / math.sqrt(times * NEIG * NSPIN / NBLOCK)
     own_rows, line = pl.pallas_call(

time: 39.3 us -> 34.5 us (0.88)
  blocking collectives: 19.1 us -> 0 us
  starting transfers between devices: 3.26 us -> 18.1 us
  local copies, waits for them, and re-layouts: 4.69 us -> 3.33 us
  Pallas kernels: 3.5 us -> 4.34 us
    all_to_all x1 -> x0, blocking collectives: 19.1 us -> none  [body(): lax.all_to_all(chunks, 'slab', split_axis=0, concat_axis=0, tiled=True)]
    ppermute x0 -> x7, starting transfers between devices: none -> 12.4 us  [body(): lax.ppermute(chunk, 'slab', [(i, i ^ partner) for i in range(count)])]
    all_to_all x1, starting transfers between devices: 3.26 us -> 5.7 us  [body(): lax.all_to_all(parts.reshape(times * count, 8, 128), ('tm', 'slab'), spli...]
    unnamed x8, local copies, waits for them, and re-layouts: 4.69 us -> 3.33 us
    pallas_call x2 -> x3, Pallas kernels: 2.76 us -> 3.6 us  [the longest x1 2.69 us: body(): pl.pallas_call(functools.partial(project_kernel, partners), out_shape=jax...]
  transfers between devices with their start and end apart: 1 -> 8, of which waited for: 1 -> 1; matrix products, arithmetic and copies ran while one was open for 0% -> 0% of each run, Pallas kernels for 0% -> 2%
where the time goes in v2:
time: 34.5 us; the launch traced here: 34.3 us
  starting transfers between devices  18.1 us (52%)
  waiting for transfers between devices  7.75 us (22%)
  Pallas kernels  4.34 us (13%)
  local copies, waits for them, and re-layouts  3.33 us (10%)
  between operations  0.73 us (2%)
    ppermute x7, starting transfers between devices, body(): lax.ppermute(chunk, 'slab', [(i, i ^ partner) for i in range(count)])  12.4 us
    all_to_all x1, waiting for transfers between devices, body(): lax.all_to_all(parts.reshape(times * count, 8, 128), ('tm', 'slab'), spli...  7.73 us
    all_to_all x1, starting transfers between devices, body(): lax.all_to_all(parts.reshape(times * count, 8, 128), ('tm', 'slab'), spli...  5.7 us
    unnamed x8, local copies, waits for them, and re-layouts  3.33 us
    pallas_call x1, Pallas kernels, body(): pl.pallas_call(functools.partial(project_kernel, partners), out_shape=jax...  2.69 us
    pallas_call x1, Pallas kernels, body(): pl.pallas_call(functools.partial(finish_kernel, count, factor), out_shape...  0.74 us
  transfers between devices with their start and end apart: 8, of which 1 were waited for; matrix products, arithmetic and copies ran while one was open for 0% of the time, Pallas kernels for 2%

profile of v2, /device:TPU:0, one launch (start us, length us, event | category | flops | bytes accessed | tf_op | source)
XLA Modules:
  0.0 34.3 jit_solution(6517903266185103907)
XLA Ops:
  0.6 0.0 copy-start.1
  0.6 1.0 %copy-done.1 = f32[1,96,1024]{2,1,0:T(8,128)S(1)} copy-done((f32[1,96,1024]{2,1,0:T(8,128)S(1)}, f32[1,96,1024]{2,1,0:T(8,128)}, u32[]{:S(2)}) %copy-start.1) | copy-done | bytes 393240
  1.6 0.3 pack.1
  1.9 4.1 %collective-permute-start = (f32[96,128]{1,0:T(8,128)S(1)}, f32[96,128]{1,0:T(8,128)S(1)}, u32[]{:S(2)}, u32[]{:S(2)}) collective-permute-start(f32[96,128]{1,0:T(8,128)S(1)} %get-tuple-element.15), channel_id=1, source_target_pairs={{0,4},{1,5},{2,6},{3,7},{4,0},{5,1},{6,2},{7,3},{8,12},{9,13},{10,... | collective-permute-start | bytes 147464 | tf_op jit(solution)/shard_map/ppermute | solution.py:149
  6.0 1.3 %collective-permute-start.1 = (f32[96,128]{1,0:T(8,128)S(1)}, f32[96,128]{1,0:T(8,128)S(1)}, u32[]{:S(2)}, u32[]{:S(2)}) collective-permute-start(f32[96,128]{1,0:T(8,128)S(1)} %get-tuple-element.16), channel_id=1, source_target_pairs={{0,6},{1,7},{2,4},{3,5},{4,2},{5,3},{6,0},{7,1},{8,14},{9,15},{10,... | collective-permute-start | bytes 147464 | tf_op jit(solution)/shard_map/ppermute | solution.py:149
  7.3 2.6 %collective-permute-start.2 = (f32[96,128]{1,0:T(8,128)S(1)}, f32[96,128]{1,0:T(8,128)S(1)}, u32[]{:S(2)}, u32[]{:S(2)}) collective-permute-start(f32[96,128]{1,0:T(8,128)S(1)} %get-tuple-element.17), channel_id=1, source_target_pairs={{0,5},{1,4},{2,7},{3,6},{4,1},{5,0},{6,3},{7,2},{8,13},{9,12},{10,... | collective-permute-start | bytes 147464 | tf_op jit(solution)/shard_map/ppermute | solution.py:149
  10.0 0.9 %collective-permute-start.3 = (f32[96,128]{1,0:T(8,128)S(1)}, f32[96,128]{1,0:T(8,128)S(1)}, u32[]{:S(2)}, u32[]{:S(2)}) collective-permute-start(f32[96,128]{1,0:T(8,128)S(1)} %get-tuple-element.18), channel_id=1, source_target_pairs={{0,7},{1,6},{2,5},{3,4},{4,3},{5,2},{6,1},{7,0},{8,15},{9,14},{10,... | collective-permute-start | bytes 147464 | tf_op jit(solution)/shard_map/ppermute | solution.py:149
  10.8 1.5 %collective-permute-start.4 = (f32[96,128]{1,0:T(8,128)S(1)}, f32[96,128]{1,0:T(8,128)S(1)}, u32[]{:S(2)}, u32[]{:S(2)}) collective-permute-start(f32[96,128]{1,0:T(8,128)S(1)} %get-tuple-element.19), channel_id=1, source_target_pairs={{0,1},{1,0},{2,3},{3,2},{4,5},{5,4},{6,7},{7,6},{8,9},{9,8},{10,11... | collective-permute-start | bytes 147464 | tf_op jit(solution)/shard_map/ppermute | solution.py:149
  12.3 0.0 collective-permute-done.refs_1_
  12.3 0.9 %collective-permute-start.5 = (f32[96,128]{1,0:T(8,128)S(1)}, f32[96,128]{1,0:T(8,128)S(1)}, u32[]{:S(2)}, u32[]{:S(2)}) collective-permute-start(f32[96,128]{1,0:T(8,128)S(1)} %get-tuple-element.20), channel_id=1, source_target_pairs={{0,3},{1,2},{2,1},{3,0},{4,7},{5,6},{6,5},{7,4},{8,11},{9,10},{10,... | collective-permute-start | bytes 147464 | tf_op jit(solution)/shard_map/ppermute | solution.py:149
  13.2 0.0 collective-permute-done.1.refs_2_
  13.2 1.1 %collective-permute-start.6 = (f32[96,128]{1,0:T(8,128)S(1)}, f32[96,128]{1,0:T(8,128)S(1)}, u32[]{:S(2)}, u32[]{:S(2)}) collective-permute-start(f32[96,128]{1,0:T(8,128)S(1)} %get-tuple-element.21), channel_id=1, source_target_pairs={{0,2},{1,3},{2,0},{3,1},{4,6},{5,7},{6,4},{7,5},{8,10},{9,11},{10,... | collective-permute-start | bytes 147464 | tf_op jit(solution)/shard_map/ppermute | solution.py:149
  14.3 0.0 copy-start
  14.3 2.3 %copy-done = f32[1,2,192,3,1024]{4,2,3,1,0:T(8,128)S(1)} copy-done((f32[1,2,192,3,1024]{4,2,3,1,0:T(8,128)S(1)}, f32[1,2,192,3,1024]{4,2,3,1,0:T(8,128)}, u32[]{:S(2)}) %copy-start) | copy-done | bytes 4718616
  16.7 0.0 copy-start.2
  16.7 0.0 copy-start.3
  16.7 0.7 %split.1 = (bf16[1536,768]{1,0:T(8,128)(2,1)S(1)}, bf16[1536,768]{1,0:T(8,128)(2,1)S(1)}) custom-call(f32[2,3,192,1024]{3,2,1,0:T(8,128)S(1)} %bitcast.16), custom_call_target="tpu_custom_call" | custom-call | flops 7077888 | bytes 9437184 | tf_op jit(solution)/shard_map/split/pallas_call | solution.py:154
  17.3 0.0 collective-permute-done.2.refs_3_
  17.3 0.0 collective-permute-done.3.refs_4_
  17.4 0.0 collective-permute-done.4.refs_5_
  17.4 0.0 collective-permute-done.5.refs_6_
  17.4 0.0 collective-permute-done.6.refs_7_
  17.4 0.0 copy-done.2
  17.4 0.0 copy-done.3
  17.4 2.7 %project.1 = f32[4,8,8,128]{3,2,1,0:T(8,128)} custom-call(s32[1]{0:T(128)} %bitcast.1.index_ref, f32[96,128]{1,0:T(8,128)S(1)} %get-tuple-element.14.refs_0_, f32[96,128]{1,0:T(8,128)S(1)} %collective-permute-done.refs_1_, f32[96,128]{1,0:T(8,128)S(1)} %collective-permute-done.1.refs_2_, f32[96,128]{1,0:T(8,128)S(1)} %collective-permute-done.2.refs_3_, ...), custom_call_target="tpu_custom_call" | custom-call | tf_op jit(solution)/shard_map/project/pallas_call | solution.py:163
  20.1 5.7 %all-to-all-start = ((f32[32,8,128]{2,1,0:T(8,128)}), f32[32,8,128]{2,1,0:T(8,128)S(1)}, u32[]{:S(2)}, u32[]{:S(2)}) async-start(f32[32,8,128]{2,1,0:T(8,128)} %bitcast.8), calls=%async_computation | async-start | bytes 262144 | tf_op jit(solution)/shard_map/all_to_all | solution.py:172
  25.8 7.7 %all-to-all-done = f32[32,8,128]{2,1,0:T(8,128)S(1)} async-done(((f32[32,8,128]{2,1,0:T(8,128)}), f32[32,8,128]{2,1,0:T(8,128)S(1)}, u32[]{:S(2)}, u32[]{:S(2)}) %all-to-all-start) | async-done | bytes 131104 | tf_op jit(solution)/shard_map/all_to_all | solution.py:172
  33.5 0.7 %finish.1 = (f32[32,24]{1,0:T(8,128)}, f32[2,4,8]{2,1,0:T(4,128)}) custom-call(s32[1]{0:T(128)} %bitcast.index_ref, f32[4,8,8,128]{3,2,1,0:T(8,128)S(1)} %bitcast.17), custom_call_target="tpu_custom_call" | custom-call | tf_op jit(solution)/shard_map/finish/pallas_call | solution.py:174
Async XLA Ops:
  0.6 1.0 %copy-start.1 = (f32[1,96,1024]{2,1,0:T(8,128)S(1)}, f32[1,96,1024]{2,1,0:T(8,128)}, u32[]{:S(2)}) copy-start(f32[1,96,1024]{2,1,0:T(8,128)} %param.4) | copy-start | bytes 1179652
  1.9 10.4 %collective-permute-start = (f32[96,128]{1,0:T(8,128)S(1)}, f32[96,128]{1,0:T(8,128)S(1)}, u32[]{:S(2)}, u32[]{:S(2)}) collective-permute-start(f32[96,128]{1,0:T(8,128)S(1)} %get-tuple-element.15), channel_id=1, source_target_pairs={{0,4},{1,5},{2,6},{3,7},{4,0},{5,1},{6,2},{7,3},{8,12},{9,13},{10,... | collective-permute-start | bytes 147464 | tf_op jit(solution)/shard_map/ppermute | solution.py:149
  6.0 7.2 %collective-permute-start.1 = (f32[96,128]{1,0:T(8,128)S(1)}, f32[96,128]{1,0:T(8,128)S(1)}, u32[]{:S(2)}, u32[]{:S(2)}) collective-permute-start(f32[96,128]{1,0:T(8,128)S(1)} %get-tuple-element.16), channel_id=1, source_target_pairs={{0,6},{1,7},{2,4},{3,5},{4,2},{5,3},{6,0},{7,1},{8,14},{9,15},{10,... | collective-permute-start | bytes 147464 | tf_op jit(solution)/shard_map/ppermute | solution.py:149
  7.3 10.0 %collective-permute-start.2 = (f32[96,128]{1,0:T(8,128)S(1)}, f32[96,128]{1,0:T(8,128)S(1)}, u32[]{:S(2)}, u32[]{:S(2)}) collective-permute-start(f32[96,128]{1,0:T(8,128)S(1)} %get-tuple-element.17), channel_id=1, source_target_pairs={{0,5},{1,4},{2,7},{3,6},{4,1},{5,0},{6,3},{7,2},{8,13},{9,12},{10,... | collective-permute-start | bytes 147464 | tf_op jit(solution)/shard_map/ppermute | solution.py:149
  10.0 7.4 %collective-permute-start.3 = (f32[96,128]{1,0:T(8,128)S(1)}, f32[96,128]{1,0:T(8,128)S(1)}, u32[]{:S(2)}, u32[]{:S(2)}) collective-permute-start(f32[96,128]{1,0:T(8,128)S(1)} %get-tuple-element.18), channel_id=1, source_target_pairs={{0,7},{1,6},{2,5},{3,4},{4,3},{5,2},{6,1},{7,0},{8,15},{9,14},{10,... | collective-permute-start | bytes 147464 | tf_op jit(solution)/shard_map/ppermute | solution.py:149
  10.8 6.5 %collective-permute-start.4 = (f32[96,128]{1,0:T(8,128)S(1)}, f32[96,128]{1,0:T(8,128)S(1)}, u32[]{:S(2)}, u32[]{:S(2)}) collective-permute-start(f32[96,128]{1,0:T(8,128)S(1)} %get-tuple-element.19), channel_id=1, source_target_pairs={{0,1},{1,0},{2,3},{3,2},{4,5},{5,4},{6,7},{7,6},{8,9},{9,8},{10,11... | collective-permute-start | bytes 147464 | tf_op jit(solution)/shard_map/ppermute | solution.py:149
  12.3 5.0 %collective-permute-start.5 = (f32[96,128]{1,0:T(8,128)S(1)}, f32[96,128]{1,0:T(8,128)S(1)}, u32[]{:S(2)}, u32[]{:S(2)}) collective-permute-start(f32[96,128]{1,0:T(8,128)S(1)} %get-tuple-element.20), channel_id=1, source_target_pairs={{0,3},{1,2},{2,1},{3,0},{4,7},{5,6},{6,5},{7,4},{8,11},{9,10},{10,... | collective-permute-start | bytes 147464 | tf_op jit(solution)/shard_map/ppermute | solution.py:149
  13.2 4.2 %collective-permute-start.6 = (f32[96,128]{1,0:T(8,128)S(1)}, f32[96,128]{1,0:T(8,128)S(1)}, u32[]{:S(2)}, u32[]{:S(2)}) collective-permute-start(f32[96,128]{1,0:T(8,128)S(1)} %get-tuple-element.21), channel_id=1, source_target_pairs={{0,2},{1,3},{2,0},{3,1},{4,6},{5,7},{6,4},{7,5},{8,10},{9,11},{10,... | collective-permute-start | bytes 147464 | tf_op jit(solution)/shard_map/ppermute | solution.py:149
  14.3 2.3 %copy-start = (f32[1,2,192,3,1024]{4,2,3,1,0:T(8,128)S(1)}, f32[1,2,192,3,1024]{4,2,3,1,0:T(8,128)}, u32[]{:S(2)}) copy-start(f32[1,2,192,3,1024]{4,2,3,1,0:T(8,128)} %param.5) | copy-start | bytes 14155780
  16.7 0.7 %copy-start.2 = (s32[192,1,4]{0,2,1:T(4,128)S(1)}, s32[192,1,4]{0,2,1:T(4,128)}, u32[]{:S(2)}) copy-start(s32[192,1,4]{0,2,1:T(4,128)} %param.6) | copy-start | bytes 9220
  16.7 0.7 %copy-start.3 = (s32[192]{0:T(256)S(1)}, s32[192]{0:T(256)}, u32[]{:S(2)}) copy-start(s32[192]{0:T(256)} %param.7) | copy-start | bytes 2308
  20.1 13.4 %all-to-all-start = ((f32[32,8,128]{2,1,0:T(8,128)}), f32[32,8,128]{2,1,0:T(8,128)S(1)}, u32[]{:S(2)}, u32[]{:S(2)}) async-start(f32[32,8,128]{2,1,0:T(8,128)} %bitcast.8), calls=%async_computation | async-start | bytes 262144 | tf_op jit(solution)/shard_map/all_to_all | solution.py:172

commit v3 on v2

--- a/solution.py
+++ b/solution.py
@@ -29,7 +29,7 @@
     return high, low
 
 
-def pack_kernel(partners, index_ref, sol_ref, *refs):
+def pack_kernel(partners, index_ref, time_ref, sol_ref, *refs):
     out_refs, (tiles, turned) = refs[: len(partners)], refs[len(partners) :]
     count = len(partners)
     width = sol_ref.shape[1] // GROUPS
@@ -48,16 +48,23 @@
             out_ref[pl.ds(color * rows, rows), :] = turned[pl.ds(r, rows, stride=count), :]
 
 
-def split_kernel(vec_ref, high_ref, low_ref):
+def split_kernel(vec_ref, high_ref, low_ref, landed, arrived):
     width = vec_ref.shape[3] // GROUPS
-    for part in range(2):
+    steps = [(part, color) for color in range(NCOLOR) for part in range(2)]
+    copies = [
+        pltpu.make_async_copy(vec_ref.at[part, color], landed.at[part, color], arrived.at[i])
+        for i, (part, color) in enumerate(steps)
+    ]
+    for copy in copies:
+        copy.start()
+    for copy, (part, color) in zip(copies, steps):
+        copy.wait()
         for g in range(GROUPS):
-            rows = pl.ds((part * GROUPS + g) * NEIG, NEIG)
-            for color in range(NCOLOR):
-                lanes = pl.ds(color * width, width)
-                high, low = split(vec_ref[part, color, :, pl.ds(g * width, width)])
-                high_ref[rows, lanes] = high
-                low_ref[rows, lanes] = low
+            rows = pl.ds((g * 2 + part) * NEIG, NEIG)
+            lanes = pl.ds(color * width, width)
+            high, low = split(landed[part, color, :, pl.ds(g * width, width)])
+            high_ref[rows, lanes] = high
+            low_ref[rows, lanes] = low
 
 
 def project_kernel(partners, index_ref, *refs):
@@ -71,25 +78,18 @@
         s = jnp.bitwise_xor(index_ref[0], partner)
         for color in range(NCOLOR):
             weights[pl.ds(color * width + s, rows, stride=count), :] = field_ref[pl.ds(color * rows, rows), :]
-    high, low = split(weights[...])
-    first = jnp.dot(high_ref[...], jnp.concatenate([high, low], axis=1), preferred_element_type=jnp.float32)
-    second = jnp.dot(low_ref[...], high, preferred_element_type=jnp.float32)
-    products = first[:, :128] + (first[:, 128:] + second)
-    lane = lax.broadcasted_iota(jnp.int32, (NEIG, 128), 1)
-    sums = []
-    for part in range(2):
-        total = products[part * GROUPS * NEIG :][:NEIG]
-        for g in range(1, GROUPS):
-            total = jnp.where(lane // COLS == g, products[(part * GROUPS + g) * NEIG :][:NEIG], total)
-        shift = 64
-        while shift >= COLS:
-            total = total + pltpu.roll(total, shift, axis=1)
-            shift //= 2
-        sums.append(total)
-    swapped = pltpu.roll(sums[1], PAIRS, axis=1)
-    product = sums[0] + jnp.where(lane % COLS < PAIRS, swapped, -swapped)
-    turned = product.T[:COLS]
-    real, imag = turned[:PAIRS], turned[PAIRS:]
+    high, low = split(weights[...].T)
+    dims = (((1,), (1,)), ((), ()))
+    total = jnp.zeros((COLS, 2 * NEIG), jnp.float32)
+    for g in range(GROUPS):
+        vecs, columns = pl.ds(g * 2 * NEIG, 2 * NEIG), slice(g * COLS, (g + 1) * COLS)
+        both = jnp.concatenate([high[columns], low[columns]], axis=0)
+        first = lax.dot_general(both, high_ref[vecs, :], dims, preferred_element_type=jnp.float32)
+        second = lax.dot_general(high[columns], low_ref[vecs, :], dims, preferred_element_type=jnp.float32)
+        total += first[:COLS] + (first[COLS:] + second)
+    with_real, with_imag = total[:, :NEIG], total[:, NEIG:]
+    real = with_real[:PAIRS] + with_imag[PAIRS:]
+    imag = with_real[PAIRS:] - with_imag[:PAIRS]
     noise = jnp.concatenate(
         [jnp.broadcast_to(noise_ref[pl.ds(spin, 1), :], (NSPIN, NEIG)) for spin in range(NSPIN)], axis=0
     )
@@ -99,12 +99,12 @@
     blocks = lax.broadcasted_iota(jnp.int32, (NBLOCK, NEIG), 0)
     onehot = (blocks == block_ref[...]).astype(jnp.bfloat16)
     line_high, line_low = split(line)
-    dims = (((1,), (1,)), ((), ()))
     line_sum = lax.dot_general(onehot, line_high, dims, preferred_element_type=jnp.float32)
     line_sum += lax.dot_general(onehot, line_low, dims, preferred_element_type=jnp.float32)
+    sums = jnp.concatenate([real, imag], axis=0)
     packed = [None] * count
     for j in range(count):
-        pieces = [turned[8 * i : 8 * i + 8, per * j : per * (j + 1)] for i in range(COLS // 8)]
+        pieces = [sums[8 * i : 8 * i + 8, per * j : per * (j + 1)] for i in range(COLS // 8)]
         used = per * len(pieces)
         if used < LINE_LANE:
             pieces.append(jnp.zeros((8, LINE_LANE - used), jnp.float32))
@@ -134,17 +134,18 @@
     per = NEIG // count
     f32 = jnp.float32
     index = lax.axis_index("slab").reshape(1)
+    time = lax.axis_index("tm").reshape(1)
     far = [p for p in ORDER if p < count]
     partners = [0] + far + [p for p in range(1, count) if p not in far]
     chunks = pl.pallas_call(
         functools.partial(pack_kernel, partners),
         out_shape=[jax.ShapeDtypeStruct((rows, 128), f32)] * count,
-        in_specs=[SMEM, VMEM],
+        in_specs=[SMEM, SMEM, VMEM],
         out_specs=[VMEM] * count,
         scratch_shapes=[pltpu.VMEM((sites // 128, NCOLOR * COLS, 128), f32), pltpu.VMEM((sites // GROUPS, 128), f32)],
         compiler_params=pltpu.CompilerParams(vmem_limit_bytes=8 * 1024 * 1024),
         name="pack",
-    )(index, solutions.reshape(solutions.shape[1:]))
+    )(index, time, solutions.reshape(solutions.shape[1:]))
     received = [
         lax.ppermute(chunk, "slab", [(i, i ^ partner) for i in range(count)]) if partner else chunk
         for partner, chunk in zip(partners, chunks)
@@ -154,15 +155,16 @@
     high, low = pl.pallas_call(
         split_kernel,
         out_shape=(shape, shape),
-        in_specs=[VMEM],
+        in_specs=[pl.BlockSpec(memory_space=pltpu.HBM)],
         out_specs=(VMEM, VMEM),
+        scratch_shapes=[pltpu.VMEM(vectors.shape, f32), pltpu.SemaphoreType.DMA((2 * NCOLOR,))],
         compiler_params=pltpu.CompilerParams(vmem_limit_bytes=24 * 1024 * 1024),
         cost_estimate=pl.CostEstimate(flops=6 * eigvecs.size, bytes_accessed=8 * eigvecs.size, transcendentals=0),
         name="split",
-    )(vectors)
+    )(pltpu.with_memory_space_constraint(vectors, pltpu.HBM))
     parts = pl.pallas_call(
         functools.partial(project_kernel, partners),
-        out_shape=jax.ShapeDtypeStruct((times, count, 8, 128), f32),
+        out_shape=pltpu.VMEM((times, count, 8, 128), f32),
         in_specs=[SMEM] + [VMEM] * (count + 4),
         out_specs=VMEM,
         scratch_shapes=[pltpu.VMEM((NCOLOR * sites // GROUPS, 128), f32)],
@@ -178,7 +180,7 @@
         out_specs=(VMEM, VMEM),
         compiler_params=pltpu.CompilerParams(vmem_limit_bytes=8 * 1024 * 1024),
         name="finish",
-    )(lax.axis_index("tm").reshape(1), parts.reshape(times, count, 8, 128))
+    )(time, parts.reshape(times, count, 8, 128))
     projected = jnp.transpose(own_rows).reshape(per, 1, 2, PAIRS)
     return projected, jnp.transpose(line, (0, 2, 1))
 

time: 34.5 us -> 33.2 us (0.962)
  blocking collectives: 0 us -> 13.1 us
  waiting for transfers between devices: 7.75 us -> 0.5 us
  starting transfers between devices: 18.1 us -> 12.4 us
  local copies, waits for them, and re-layouts: 3.33 us -> 1 us
  Pallas kernels: 4.34 us -> 5.33 us
    all_to_all x0 -> x1, blocking collectives: none -> 13.1 us  [body(): lax.all_to_all(parts.reshape(times * count, 8, 128), ('tm', 'slab'), spli...]
    all_to_all x1 -> x0, waiting for transfers between devices: 7.73 us -> none  [body(): lax.all_to_all(parts.reshape(times * count, 8, 128), ('tm', 'slab'), spli...]
    all_to_all x1 -> x0, starting transfers between devices: 5.7 us -> none  [body(): lax.all_to_all(parts.reshape(times * count, 8, 128), ('tm', 'slab'), spli...]
    unnamed x8 -> x6, local copies, waits for them, and re-layouts: 3.33 us -> 1 us
    pallas_call x2, Pallas kernels: 3.34 us -> 4.34 us  [the longest x1 2.51 us: body(): pl.pallas_call(split_kernel, out_shape=(shape, shape), in_specs=[pl.Block...]
    ppermute x7, waiting for transfers between devices: 0.02 us -> 0.5 us  [body(): lax.ppermute(chunk, 'slab', [(i, i ^ partner) for i in range(count)])]
  transfers between devices with their start and end apart: 8 -> 7, of which waited for: 1 -> 1; matrix products, arithmetic and copies ran while one was open for 0% -> 0% of each run, Pallas kernels for 2% -> 8%
where the time goes in v3:
time: 33.2 us; the launch traced here: 33 us
  blocking collectives  13.1 us (39%)
  starting transfers between devices  12.4 us (37%)
  Pallas kernels  5.33 us (16%)
  local copies, waits for them, and re-layouts  1 us (3%)
  between operations  0.7 us (2%)
  waiting for transfers between devices  0.5 us (2%)
    all_to_all x1, blocking collectives, body(): lax.all_to_all(parts.reshape(times * count, 8, 128), ('tm', 'slab'), spli...  13.1 us
    ppermute x7, starting transfers between devices, body(): lax.ppermute(chunk, 'slab', [(i, i ^ partner) for i in range(count)])  12.4 us
    pallas_call x1, Pallas kernels, body(): pl.pallas_call(split_kernel, out_shape=(shape, shape), in_specs=[pl.Block...  2.51 us
    pallas_call x1, Pallas kernels, body(): pl.pallas_call(functools.partial(project_kernel, partners), out_shape=plt...  1.83 us
    unnamed x6, local copies, waits for them, and re-layouts  1 us
    pallas_call x1, Pallas kernels, body(): pl.pallas_call(functools.partial(finish_kernel, count, factor), out_shape...  0.74 us
  transfers between devices with their start and end apart: 7, of which 1 were waited for; matrix products, arithmetic and copies ran while one was open for 0% of the time, Pallas kernels for 8%

profile of v3, /device:TPU:0, one launch (start us, length us, event | category | flops | bytes accessed | tf_op | source)
XLA Modules:
  0.0 33.0 jit_solution(15668790831267515493)
XLA Ops:
  0.6 0.0 copy-start
  0.6 1.0 %copy-done = f32[1,96,1024]{2,1,0:T(8,128)S(1)} copy-done((f32[1,96,1024]{2,1,0:T(8,128)S(1)}, f32[1,96,1024]{2,1,0:T(8,128)}, u32[]{:S(2)}) %copy-start) | copy-done | bytes 393240
  1.6 0.3 pack.1
  1.9 4.1 %collective-permute-start = (f32[96,128]{1,0:T(8,128)S(1)}, f32[96,128]{1,0:T(8,128)S(1)}, u32[]{:S(2)}, u32[]{:S(2)}) collective-permute-start(f32[96,128]{1,0:T(8,128)S(1)} %get-tuple-element.15), channel_id=1, source_target_pairs={{0,4},{1,5},{2,6},{3,7},{4,0},{5,1},{6,2},{7,3},{8,12},{9,13},{10,... | collective-permute-start | bytes 147464 | tf_op jit(solution)/shard_map/ppermute | solution.py:150
  6.0 1.3 %collective-permute-start.1 = (f32[96,128]{1,0:T(8,128)S(1)}, f32[96,128]{1,0:T(8,128)S(1)}, u32[]{:S(2)}, u32[]{:S(2)}) collective-permute-start(f32[96,128]{1,0:T(8,128)S(1)} %get-tuple-element.16), channel_id=1, source_target_pairs={{0,6},{1,7},{2,4},{3,5},{4,2},{5,3},{6,0},{7,1},{8,14},{9,15},{10,... | collective-permute-start | bytes 147464 | tf_op jit(solution)/shard_map/ppermute | solution.py:150
  7.3 2.6 %collective-permute-start.2 = (f32[96,128]{1,0:T(8,128)S(1)}, f32[96,128]{1,0:T(8,128)S(1)}, u32[]{:S(2)}, u32[]{:S(2)}) collective-permute-start(f32[96,128]{1,0:T(8,128)S(1)} %get-tuple-element.17), channel_id=1, source_target_pairs={{0,5},{1,4},{2,7},{3,6},{4,1},{5,0},{6,3},{7,2},{8,13},{9,12},{10,... | collective-permute-start | bytes 147464 | tf_op jit(solution)/shard_map/ppermute | solution.py:150
  10.0 0.9 %collective-permute-start.3 = (f32[96,128]{1,0:T(8,128)S(1)}, f32[96,128]{1,0:T(8,128)S(1)}, u32[]{:S(2)}, u32[]{:S(2)}) collective-permute-start(f32[96,128]{1,0:T(8,128)S(1)} %get-tuple-element.18), channel_id=1, source_target_pairs={{0,7},{1,6},{2,5},{3,4},{4,3},{5,2},{6,1},{7,0},{8,15},{9,14},{10,... | collective-permute-start | bytes 147464 | tf_op jit(solution)/shard_map/ppermute | solution.py:150
  10.8 1.5 %collective-permute-start.4 = (f32[96,128]{1,0:T(8,128)S(1)}, f32[96,128]{1,0:T(8,128)S(1)}, u32[]{:S(2)}, u32[]{:S(2)}) collective-permute-start(f32[96,128]{1,0:T(8,128)S(1)} %get-tuple-element.19), channel_id=1, source_target_pairs={{0,1},{1,0},{2,3},{3,2},{4,5},{5,4},{6,7},{7,6},{8,9},{9,8},{10,11... | collective-permute-start | bytes 147464 | tf_op jit(solution)/shard_map/ppermute | solution.py:150
  12.3 0.0 collective-permute-done.refs_1_
  12.3 0.9 %collective-permute-start.5 = (f32[96,128]{1,0:T(8,128)S(1)}, f32[96,128]{1,0:T(8,128)S(1)}, u32[]{:S(2)}, u32[]{:S(2)}) collective-permute-start(f32[96,128]{1,0:T(8,128)S(1)} %get-tuple-element.20), channel_id=1, source_target_pairs={{0,3},{1,2},{2,1},{3,0},{4,7},{5,6},{6,5},{7,4},{8,11},{9,10},{10,... | collective-permute-start | bytes 147464 | tf_op jit(solution)/shard_map/ppermute | solution.py:150
  13.2 0.0 collective-permute-done.1.refs_2_
  13.2 1.1 %collective-permute-start.6 = (f32[96,128]{1,0:T(8,128)S(1)}, f32[96,128]{1,0:T(8,128)S(1)}, u32[]{:S(2)}, u32[]{:S(2)}) collective-permute-start(f32[96,128]{1,0:T(8,128)S(1)} %get-tuple-element.21), channel_id=1, source_target_pairs={{0,2},{1,3},{2,0},{3,1},{4,6},{5,7},{6,4},{7,5},{8,10},{9,11},{10,... | collective-permute-start | bytes 147464 | tf_op jit(solution)/shard_map/ppermute | solution.py:150
  14.3 0.0 copy-start.1
  14.3 0.0 copy-start.2
  14.3 2.5 %split.1 = (bf16[1536,768]{1,0:T(8,128)(2,1)S(1)}, bf16[1536,768]{1,0:T(8,128)(2,1)S(1)}) custom-call(f32[2,3,192,1024]{3,2,1,0:T(8,128)} %bitcast.21), custom_call_target="tpu_custom_call" | custom-call | flops 7077888 | bytes 9437184 | tf_op jit(solution)/shard_map/split/pallas_call | solution.py:155
  16.9 0.0 collective-permute-done.2.refs_3_
  16.9 0.0 collective-permute-done.3.refs_4_
  16.9 0.0 collective-permute-done.4.refs_5_
  16.9 0.5 %collective-permute-done.5.refs_6_ = f32[96,128]{1,0:T(8,128)S(1)} collective-permute-done((f32[96,128]{1,0:T(8,128)S(1)}, f32[96,128]{1,0:T(8,128)S(1)}, u32[]{:S(2)}, u32[]{:S(2)}) %collective-permute-start.5) | collective-permute-done | bytes 49184 | tf_op jit(solution)/shard_map/ppermute | solution.py:150
  17.4 0.0 collective-permute-done.6.refs_7_
  17.4 0.0 copy-done.1
  17.4 0.0 copy-done.2
  17.4 1.8 %project.1 = f32[4,8,8,128]{3,2,1,0:T(8,128)S(1)} custom-call(s32[1]{0:T(128)} %bitcast.1.index_ref, f32[96,128]{1,0:T(8,128)S(1)} %get-tuple-element.14.refs_0_, f32[96,128]{1,0:T(8,128)S(1)} %collective-permute-done.refs_1_, f32[96,128]{1,0:T(8,128)S(1)} %collective-permute-done.1.refs_2_, f32[96,128]{1,0:T(8,128)S(1)} %collective-permute-done.2.refs_3_, ...), custom_call_target="tpu_custom_call" | custom-call | tf_op jit(solution)/shard_map/project/pallas_call | solution.py:165
  19.2 13.1 %all_to_all.5 = f32[32,8,128]{2,1,0:T(8,128)S(1)} all-to-all(f32[32,8,128]{2,1,0:T(8,128)S(1)} %bitcast.17), channel_id=1, replica_groups=mesh['tm'=4,'slab'=8] {'tm','slab'}, dimensions={0} | all-to-all | bytes 262144 | tf_op jit(solution)/shard_map/all_to_all | solution.py:174
  32.3 0.7 %finish.1 = (f32[32,24]{1,0:T(8,128)}, f32[2,4,8]{2,1,0:T(4,128)}) custom-call(s32[1]{0:T(128)} %bitcast.time_ref.index_ref, f32[4,8,8,128]{3,2,1,0:T(8,128)S(1)} %bitcast.16), custom_call_target="tpu_custom_call" | custom-call | tf_op jit(solution)/shard_map/finish/pallas_call | solution.py:176
Async XLA Ops:
  0.6 1.0 %copy-start = (f32[1,96,1024]{2,1,0:T(8,128)S(1)}, f32[1,96,1024]{2,1,0:T(8,128)}, u32[]{:S(2)}) copy-start(f32[1,96,1024]{2,1,0:T(8,128)} %param.4) | copy-start | bytes 1179652
  1.9 10.4 %collective-permute-start = (f32[96,128]{1,0:T(8,128)S(1)}, f32[96,128]{1,0:T(8,128)S(1)}, u32[]{:S(2)}, u32[]{:S(2)}) collective-permute-start(f32[96,128]{1,0:T(8,128)S(1)} %get-tuple-element.15), channel_id=1, source_target_pairs={{0,4},{1,5},{2,6},{3,7},{4,0},{5,1},{6,2},{7,3},{8,12},{9,13},{10,... | collective-permute-start | bytes 147464 | tf_op jit(solution)/shard_map/ppermute | solution.py:150
  6.0 7.2 %collective-permute-start.1 = (f32[96,128]{1,0:T(8,128)S(1)}, f32[96,128]{1,0:T(8,128)S(1)}, u32[]{:S(2)}, u32[]{:S(2)}) collective-permute-start(f32[96,128]{1,0:T(8,128)S(1)} %get-tuple-element.16), channel_id=1, source_target_pairs={{0,6},{1,7},{2,4},{3,5},{4,2},{5,3},{6,0},{7,1},{8,14},{9,15},{10,... | collective-permute-start | bytes 147464 | tf_op jit(solution)/shard_map/ppermute | solution.py:150
  7.3 9.5 %collective-permute-start.2 = (f32[96,128]{1,0:T(8,128)S(1)}, f32[96,128]{1,0:T(8,128)S(1)}, u32[]{:S(2)}, u32[]{:S(2)}) collective-permute-start(f32[96,128]{1,0:T(8,128)S(1)} %get-tuple-element.17), channel_id=1, source_target_pairs={{0,5},{1,4},{2,7},{3,6},{4,1},{5,0},{6,3},{7,2},{8,13},{9,12},{10,... | collective-permute-start | bytes 147464 | tf_op jit(solution)/shard_map/ppermute | solution.py:150
  10.0 6.9 %collective-permute-start.3 = (f32[96,128]{1,0:T(8,128)S(1)}, f32[96,128]{1,0:T(8,128)S(1)}, u32[]{:S(2)}, u32[]{:S(2)}) collective-permute-start(f32[96,128]{1,0:T(8,128)S(1)} %get-tuple-element.18), channel_id=1, source_target_pairs={{0,7},{1,6},{2,5},{3,4},{4,3},{5,2},{6,1},{7,0},{8,15},{9,14},{10,... | collective-permute-start | bytes 147464 | tf_op jit(solution)/shard_map/ppermute | solution.py:150
  10.8 6.0 %collective-permute-start.4 = (f32[96,128]{1,0:T(8,128)S(1)}, f32[96,128]{1,0:T(8,128)S(1)}, u32[]{:S(2)}, u32[]{:S(2)}) collective-permute-start(f32[96,128]{1,0:T(8,128)S(1)} %get-tuple-element.19), channel_id=1, source_target_pairs={{0,1},{1,0},{2,3},{3,2},{4,5},{5,4},{6,7},{7,6},{8,9},{9,8},{10,11... | collective-permute-start | bytes 147464 | tf_op jit(solution)/shard_map/ppermute | solution.py:150
  12.3 5.0 %collective-permute-start.5 = (f32[96,128]{1,0:T(8,128)S(1)}, f32[96,128]{1,0:T(8,128)S(1)}, u32[]{:S(2)}, u32[]{:S(2)}) collective-permute-start(f32[96,128]{1,0:T(8,128)S(1)} %get-tuple-element.20), channel_id=1, source_target_pairs={{0,3},{1,2},{2,1},{3,0},{4,7},{5,6},{6,5},{7,4},{8,11},{9,10},{10,... | collective-permute-start | bytes 147464 | tf_op jit(solution)/shard_map/ppermute | solution.py:150
  13.2 4.2 %collective-permute-start.6 = (f32[96,128]{1,0:T(8,128)S(1)}, f32[96,128]{1,0:T(8,128)S(1)}, u32[]{:S(2)}, u32[]{:S(2)}) collective-permute-start(f32[96,128]{1,0:T(8,128)S(1)} %get-tuple-element.21), channel_id=1, source_target_pairs={{0,2},{1,3},{2,0},{3,1},{4,6},{5,7},{6,4},{7,5},{8,10},{9,11},{10,... | collective-permute-start | bytes 147464 | tf_op jit(solution)/shard_map/ppermute | solution.py:150
  14.3 3.0 %copy-start.1 = (s32[192,1,4]{0,2,1:T(4,128)S(1)}, s32[192,1,4]{0,2,1:T(4,128)}, u32[]{:S(2)}) copy-start(s32[192,1,4]{0,2,1:T(4,128)} %param.6) | copy-start | bytes 9220
  14.3 3.0 %copy-start.2 = (s32[192]{0:T(256)S(1)}, s32[192]{0:T(256)}, u32[]{:S(2)}) copy-start(s32[192]{0:T(256)} %param.7) | copy-start | bytes 2308

commit v4 on v3

--- a/solution.py
+++ b/solution.py
@@ -15,6 +15,7 @@
 PAIRS = NSPIN * NSPIN
 COLS = 2 * PAIRS
 GROUPS = 128 // COLS
+CORES = 2
 LINE_LANE = 96
 
 ORDER = (4, 6, 5, 7, 1, 3, 2)
@@ -70,7 +71,7 @@
 def project_kernel(partners, index_ref, *refs):
     count = len(partners)
     field_refs = refs[:count]
-    high_ref, low_ref, noise_ref, block_ref, out_ref, weights = refs[count:]
+    high_ref, low_ref, noise_ref, block_ref, out_ref, line_ref, weights = refs[count:]
     width = high_ref.shape[1] // NCOLOR
     rows = width // count
     per = NEIG // count
@@ -102,21 +103,25 @@
     line_sum = lax.dot_general(onehot, line_high, dims, preferred_element_type=jnp.float32)
     line_sum += lax.dot_general(onehot, line_low, dims, preferred_element_type=jnp.float32)
     sums = jnp.concatenate([real, imag], axis=0)
-    packed = [None] * count
+    lines = jnp.concatenate([jnp.zeros((8, LINE_LANE), jnp.float32), line_sum], axis=1)
+    line_ref[...] = lines
     for j in range(count):
         pieces = [sums[8 * i : 8 * i + 8, per * j : per * (j + 1)] for i in range(COLS // 8)]
-        used = per * len(pieces)
-        if used < LINE_LANE:
-            pieces.append(jnp.zeros((8, LINE_LANE - used), jnp.float32))
-        packed[j] = jnp.concatenate(pieces + [line_sum], axis=1)
-    for i in range(out_ref.shape[0]):
-        for j in range(count):
-            out_ref[i, j] = packed[j]
+        pieces.append(jnp.zeros((8, 128 - per * len(pieces)), jnp.float32))
+        out_ref[j] = jnp.concatenate(pieces, axis=1) + lines
+
+
+def join_kernel(part_ref, line_ref, out_ref):
+    count = part_ref.shape[0]
+    for j in range(count):
+        part = part_ref[j] + line_ref[...]
+        for i in range(out_ref.shape[0]):
+            out_ref[i, count - 1 - j] = part
 
 
 def finish_kernel(count, factor, index_ref, parts_ref, rows_ref, line_ref):
     per = NEIG // count
-    own = jnp.sum(parts_ref[index_ref[0]], axis=0)
+    own = jnp.sum(parts_ref[parts_ref.shape[0] - 1 - index_ref[0] // CORES], axis=0)
     for i in range(COLS // 8):
         rows_ref[pl.ds(8 * i, 8), :] = own[:, per * i : per * (i + 1)]
     whole = jnp.sum(jnp.sum(parts_ref[...], axis=1), axis=0)
@@ -162,16 +167,32 @@
         cost_estimate=pl.CostEstimate(flops=6 * eigvecs.size, bytes_accessed=8 * eigvecs.size, transcendentals=0),
         name="split",
     )(pltpu.with_memory_space_constraint(vectors, pltpu.HBM))
-    parts = pl.pallas_call(
+    part, line = pl.pallas_call(
         functools.partial(project_kernel, partners),
-        out_shape=pltpu.VMEM((times, count, 8, 128), f32),
+        out_shape=(pltpu.VMEM((count, 8, 128), f32), pltpu.VMEM((8, 128), f32)),
         in_specs=[SMEM] + [VMEM] * (count + 4),
-        out_specs=VMEM,
+        out_specs=(VMEM, VMEM),
         scratch_shapes=[pltpu.VMEM((NCOLOR * sites // GROUPS, 128), f32)],
         compiler_params=pltpu.CompilerParams(vmem_limit_bytes=24 * 1024 * 1024),
         name="project",
     )(index, *received, high, low, jnp.transpose(sink_noise.reshape(NEIG, NSPIN)), eig_block.reshape(1, NEIG))
-    parts = lax.all_to_all(parts.reshape(times * count, 8, 128), ("tm", "slab"), split_axis=0, concat_axis=0, tiled=True)
+    line = lax.ppermute(line, "tm", [(i, i ^ 1) for i in range(times)])
+    chips = times // CORES
+    parts = pl.pallas_call(
+        join_kernel,
+        out_shape=pltpu.VMEM((chips, count, 8, 128), f32),
+        in_specs=[VMEM, VMEM],
+        out_specs=VMEM,
+        compiler_params=pltpu.CompilerParams(vmem_limit_bytes=8 * 1024 * 1024),
+        name="join",
+    )(part, line)
+    groups = [
+        [(chip * CORES + core) * count + s for chip in reversed(range(chips)) for s in reversed(range(count))]
+        for core in range(CORES)
+    ]
+    parts = lax.all_to_all(
+        parts.reshape(chips * count, 8, 128), ("tm", "slab"), 0, 0, axis_index_groups=groups, tiled=True
+    )
     factor = 1.0 / math.sqrt(times * NEIG * NSPIN / NBLOCK)
     own_rows, line = pl.pallas_call(
         functools.partial(finish_kernel, count, factor),
@@ -180,7 +201,7 @@
         out_specs=(VMEM, VMEM),
         compiler_params=pltpu.CompilerParams(vmem_limit_bytes=8 * 1024 * 1024),
         name="finish",
-    )(time, parts.reshape(times, count, 8, 128))
+    )(time, parts.reshape(chips, count, 8, 128))
     projected = jnp.transpose(own_rows).reshape(per, 1, 2, PAIRS)
     return projected, jnp.transpose(line, (0, 2, 1))
 

time: 33.2 us -> 32.4 us (0.976)
  blocking collectives: 13.1 us -> 11.1 us
  waiting for transfers between devices: 0.5 us -> 1.66 us
    all_to_all x1, blocking collectives: 13.1 us -> 11.1 us  [body(): lax.all_to_all(parts.reshape(chips * count, 8, 128), ('tm', 'slab'), 0, 0...]
    ppermute x0 -> x1, waiting for transfers between devices: none -> 1.16 us  [body(): line = lax.ppermute(line, 'tm', [(i, i ^ 1) for i in range(times)])]
    pallas_call x1 -> x2, Pallas kernels: 1.83 us -> 1.82 us  [the longest x1 1.81 us: body(): pl.pallas_call(functools.partial(project_kernel, partners), out_shape=(pl...]
  transfers between devices with their start and end apart: 7 -> 8, of which waited for: 1 -> 2; matrix products, arithmetic and copies ran while one was open for 0% -> 0% of each run, Pallas kernels for 8% -> 8%
where the time goes in v4:
time: 32.4 us; the launch traced here: 32.2 us
  starting transfers between devices  12.4 us (38%)
  blocking collectives  11.1 us (34%)
  Pallas kernels  5.32 us (16%)
  waiting for transfers between devices  1.66 us (5%)
  local copies, waits for them, and re-layouts  1 us (3%)
  between operations  0.7 us (2%)
    ppermute x7, starting transfers between devices, body(): lax.ppermute(chunk, 'slab', [(i, i ^ partner) for i in range(count)])  12.4 us
    all_to_all x1, blocking collectives, body(): lax.all_to_all(parts.reshape(chips * count, 8, 128), ('tm', 'slab'), 0, 0...  11.1 us
    pallas_call x1, Pallas kernels, body(): pl.pallas_call(split_kernel, out_shape=(shape, shape), in_specs=[pl.Block...  2.5 us
    pallas_call x1, Pallas kernels, body(): pl.pallas_call(functools.partial(project_kernel, partners), out_shape=(pl...  1.81 us
    ppermute x1, waiting for transfers between devices, body(): line = lax.ppermute(line, 'tm', [(i, i ^ 1) for i in range(times)])  1.16 us
    unnamed x6, local copies, waits for them, and re-layouts  1 us
    pallas_call x1, Pallas kernels, body(): pl.pallas_call(functools.partial(finish_kernel, count, factor), out_shape...  0.74 us
  transfers between devices with their start and end apart: 8, of which 2 were waited for; matrix products, arithmetic and copies ran while one was open for 0% of the time, Pallas kernels for 8%

profile of v4, /device:TPU:0, one launch (start us, length us, event | category | flops | bytes accessed | tf_op | source)
XLA Modules:
  0.0 32.2 jit_solution(17159860836395912721)
XLA Ops:
  0.6 0.0 copy-start
  0.6 1.0 %copy-done = f32[1,96,1024]{2,1,0:T(8,128)S(1)} copy-done((f32[1,96,1024]{2,1,0:T(8,128)S(1)}, f32[1,96,1024]{2,1,0:T(8,128)}, u32[]{:S(2)}) %copy-start) | copy-done | bytes 393240
  1.6 0.3 pack.1
  1.9 4.1 %collective-permute-start = (f32[96,128]{1,0:T(8,128)S(1)}, f32[96,128]{1,0:T(8,128)S(1)}, u32[]{:S(2)}, u32[]{:S(2)}) collective-permute-start(f32[96,128]{1,0:T(8,128)S(1)} %get-tuple-element.17), channel_id=1, source_target_pairs={{0,4},{1,5},{2,6},{3,7},{4,0},{5,1},{6,2},{7,3},{8,12},{9,13},{10,... | collective-permute-start | bytes 147464 | tf_op jit(solution)/shard_map/ppermute | solution.py:155
  6.0 1.3 %collective-permute-start.1 = (f32[96,128]{1,0:T(8,128)S(1)}, f32[96,128]{1,0:T(8,128)S(1)}, u32[]{:S(2)}, u32[]{:S(2)}) collective-permute-start(f32[96,128]{1,0:T(8,128)S(1)} %get-tuple-element.18), channel_id=1, source_target_pairs={{0,6},{1,7},{2,4},{3,5},{4,2},{5,3},{6,0},{7,1},{8,14},{9,15},{10,... | collective-permute-start | bytes 147464 | tf_op jit(solution)/shard_map/ppermute | solution.py:155
  7.3 2.6 %collective-permute-start.2 = (f32[96,128]{1,0:T(8,128)S(1)}, f32[96,128]{1,0:T(8,128)S(1)}, u32[]{:S(2)}, u32[]{:S(2)}) collective-permute-start(f32[96,128]{1,0:T(8,128)S(1)} %get-tuple-element.19), channel_id=1, source_target_pairs={{0,5},{1,4},{2,7},{3,6},{4,1},{5,0},{6,3},{7,2},{8,13},{9,12},{10,... | collective-permute-start | bytes 147464 | tf_op jit(solution)/shard_map/ppermute | solution.py:155
  10.0 0.9 %collective-permute-start.3 = (f32[96,128]{1,0:T(8,128)S(1)}, f32[96,128]{1,0:T(8,128)S(1)}, u32[]{:S(2)}, u32[]{:S(2)}) collective-permute-start(f32[96,128]{1,0:T(8,128)S(1)} %get-tuple-element.20), channel_id=1, source_target_pairs={{0,7},{1,6},{2,5},{3,4},{4,3},{5,2},{6,1},{7,0},{8,15},{9,14},{10,... | collective-permute-start | bytes 147464 | tf_op jit(solution)/shard_map/ppermute | solution.py:155
  10.8 1.5 %collective-permute-start.4 = (f32[96,128]{1,0:T(8,128)S(1)}, f32[96,128]{1,0:T(8,128)S(1)}, u32[]{:S(2)}, u32[]{:S(2)}) collective-permute-start(f32[96,128]{1,0:T(8,128)S(1)} %get-tuple-element.21), channel_id=1, source_target_pairs={{0,1},{1,0},{2,3},{3,2},{4,5},{5,4},{6,7},{7,6},{8,9},{9,8},{10,11... | collective-permute-start | bytes 147464 | tf_op jit(solution)/shard_map/ppermute | solution.py:155
  12.3 0.0 collective-permute-done.refs_1_
  12.3 0.9 %collective-permute-start.5 = (f32[96,128]{1,0:T(8,128)S(1)}, f32[96,128]{1,0:T(8,128)S(1)}, u32[]{:S(2)}, u32[]{:S(2)}) collective-permute-start(f32[96,128]{1,0:T(8,128)S(1)} %get-tuple-element.22), channel_id=1, source_target_pairs={{0,3},{1,2},{2,1},{3,0},{4,7},{5,6},{6,5},{7,4},{8,11},{9,10},{10,... | collective-permute-start | bytes 147464 | tf_op jit(solution)/shard_map/ppermute | solution.py:155
  13.2 0.0 collective-permute-done.1.refs_2_
  13.2 1.1 %collective-permute-start.6 = (f32[96,128]{1,0:T(8,128)S(1)}, f32[96,128]{1,0:T(8,128)S(1)}, u32[]{:S(2)}, u32[]{:S(2)}) collective-permute-start(f32[96,128]{1,0:T(8,128)S(1)} %get-tuple-element.23), channel_id=1, source_target_pairs={{0,2},{1,3},{2,0},{3,1},{4,6},{5,7},{6,4},{7,5},{8,10},{9,11},{10,... | collective-permute-start | bytes 147464 | tf_op jit(solution)/shard_map/ppermute | solution.py:155
  14.3 0.0 copy-start.1
  14.3 0.0 copy-start.2
  14.3 2.5 %split.1 = (bf16[1536,768]{1,0:T(8,128)(2,1)S(1)}, bf16[1536,768]{1,0:T(8,128)(2,1)S(1)}) custom-call(f32[2,3,192,1024]{3,2,1,0:T(8,128)} %bitcast.21), custom_call_target="tpu_custom_call" | custom-call | flops 7077888 | bytes 9437184 | tf_op jit(solution)/shard_map/split/pallas_call | solution.py:160
  16.8 0.0 collective-permute-done.2.refs_3_
  16.9 0.0 collective-permute-done.3.refs_4_
  16.9 0.0 collective-permute-done.4.refs_5_
  16.9 0.5 %collective-permute-done.5.refs_6_ = f32[96,128]{1,0:T(8,128)S(1)} collective-permute-done((f32[96,128]{1,0:T(8,128)S(1)}, f32[96,128]{1,0:T(8,128)S(1)}, u32[]{:S(2)}, u32[]{:S(2)}) %collective-permute-start.5) | collective-permute-done | bytes 49184 | tf_op jit(solution)/shard_map/ppermute | solution.py:155
  17.4 0.0 collective-permute-done.6.refs_7_
  17.4 0.0 copy-done.1
  17.4 0.0 copy-done.2
  17.4 1.8 %project.1 = (f32[8,8,128]{2,1,0:T(8,128)S(1)}, f32[8,128]{1,0:T(8,128)S(1)}) custom-call(s32[1]{0:T(128)} %bitcast.1.index_ref, f32[96,128]{1,0:T(8,128)S(1)} %get-tuple-element.16.refs_0_, f32[96,128]{1,0:T(8,128)S(1)} %collective-permute-done.refs_1_, f32[96,128]{1,0:T(8,128)S(1)} %collective-permute-done.1.refs_2_, ...), custom_call_target="tpu_custom_call" | custom-call | tf_op jit(solution)/shard_map/project/pallas_call | solution.py:170
  19.2 0.0 collective-permute-start.7
  19.2 1.2 %collective-permute-done.7.line_ref = f32[8,128]{1,0:T(8,128)S(1)} collective-permute-done((f32[8,128]{1,0:T(8,128)S(1)}, f32[8,128]{1,0:T(8,128)S(1)}, u32[]{:S(2)}, u32[]{:S(2)}) %collective-permute-start.7) | collective-permute-done | bytes 4128 | tf_op jit(solution)/shard_map/ppermute | solution.py:179
  20.4 11.1 %all_to_all.5 = f32[16,8,128]{2,1,0:T(8,128)S(1)} all-to-all(f32[16,8,128]{2,1,0:T(8,128)S(1)} %bitcast.18), channel_id=1, replica_groups={{23,22,21,20,19,18,17,16,7,6,5,4,3,2,1,0},{31,30,29,28,27,26,25,24,15,1..., dimensions={0} | all-to-all | bytes 131072 | tf_op jit(solution)/shard_map/all_to_all | solution.py:193
  31.5 0.7 %finish.1 = (f32[32,24]{1,0:T(8,128)}, f32[2,4,8]{2,1,0:T(4,128)}) custom-call(s32[1]{0:T(128)} %bitcast.time_ref.index_ref, f32[2,8,8,128]{3,2,1,0:T(8,128)S(1)} %bitcast.17), custom_call_target="tpu_custom_call" | custom-call | tf_op jit(solution)/shard_map/finish/pallas_call | solution.py:197
  (1 shorter events, 0.0 us)
Async XLA Ops:
  0.6 1.0 %copy-start = (f32[1,96,1024]{2,1,0:T(8,128)S(1)}, f32[1,96,1024]{2,1,0:T(8,128)}, u32[]{:S(2)}) copy-start(f32[1,96,1024]{2,1,0:T(8,128)} %param.4) | copy-start | bytes 1179652
  1.9 10.4 %collective-permute-start = (f32[96,128]{1,0:T(8,128)S(1)}, f32[96,128]{1,0:T(8,128)S(1)}, u32[]{:S(2)}, u32[]{:S(2)}) collective-permute-start(f32[96,128]{1,0:T(8,128)S(1)} %get-tuple-element.17), channel_id=1, source_target_pairs={{0,4},{1,5},{2,6},{3,7},{4,0},{5,1},{6,2},{7,3},{8,12},{9,13},{10,... | collective-permute-start | bytes 147464 | tf_op jit(solution)/shard_map/ppermute | solution.py:155
  6.0 7.2 %collective-permute-start.1 = (f32[96,128]{1,0:T(8,128)S(1)}, f32[96,128]{1,0:T(8,128)S(1)}, u32[]{:S(2)}, u32[]{:S(2)}) collective-permute-start(f32[96,128]{1,0:T(8,128)S(1)} %get-tuple-element.18), channel_id=1, source_target_pairs={{0,6},{1,7},{2,4},{3,5},{4,2},{5,3},{6,0},{7,1},{8,14},{9,15},{10,... | collective-permute-start | bytes 147464 | tf_op jit(solution)/shard_map/ppermute | solution.py:155
  7.3 9.5 %collective-permute-start.2 = (f32[96,128]{1,0:T(8,128)S(1)}, f32[96,128]{1,0:T(8,128)S(1)}, u32[]{:S(2)}, u32[]{:S(2)}) collective-permute-start(f32[96,128]{1,0:T(8,128)S(1)} %get-tuple-element.19), channel_id=1, source_target_pairs={{0,5},{1,4},{2,7},{3,6},{4,1},{5,0},{6,3},{7,2},{8,13},{9,12},{10,... | collective-permute-start | bytes 147464 | tf_op jit(solution)/shard_map/ppermute | solution.py:155
  10.0 6.9 %collective-permute-start.3 = (f32[96,128]{1,0:T(8,128)S(1)}, f32[96,128]{1,0:T(8,128)S(1)}, u32[]{:S(2)}, u32[]{:S(2)}) collective-permute-start(f32[96,128]{1,0:T(8,128)S(1)} %get-tuple-element.20), channel_id=1, source_target_pairs={{0,7},{1,6},{2,5},{3,4},{4,3},{5,2},{6,1},{7,0},{8,15},{9,14},{10,... | collective-permute-start | bytes 147464 | tf_op jit(solution)/shard_map/ppermute | solution.py:155
  10.8 6.0 %collective-permute-start.4 = (f32[96,128]{1,0:T(8,128)S(1)}, f32[96,128]{1,0:T(8,128)S(1)}, u32[]{:S(2)}, u32[]{:S(2)}) collective-permute-start(f32[96,128]{1,0:T(8,128)S(1)} %get-tuple-element.21), channel_id=1, source_target_pairs={{0,1},{1,0},{2,3},{3,2},{4,5},{5,4},{6,7},{7,6},{8,9},{9,8},{10,11... | collective-permute-start | bytes 147464 | tf_op jit(solution)/shard_map/ppermute | solution.py:155
  12.3 5.0 %collective-permute-start.5 = (f32[96,128]{1,0:T(8,128)S(1)}, f32[96,128]{1,0:T(8,128)S(1)}, u32[]{:S(2)}, u32[]{:S(2)}) collective-permute-start(f32[96,128]{1,0:T(8,128)S(1)} %get-tuple-element.22), channel_id=1, source_target_pairs={{0,3},{1,2},{2,1},{3,0},{4,7},{5,6},{6,5},{7,4},{8,11},{9,10},{10,... | collective-permute-start | bytes 147464 | tf_op jit(solution)/shard_map/ppermute | solution.py:155
  13.2 4.2 %collective-permute-start.6 = (f32[96,128]{1,0:T(8,128)S(1)}, f32[96,128]{1,0:T(8,128)S(1)}, u32[]{:S(2)}, u32[]{:S(2)}) collective-permute-start(f32[96,128]{1,0:T(8,128)S(1)} %get-tuple-element.23), channel_id=1, source_target_pairs={{0,2},{1,3},{2,0},{3,1},{4,6},{5,7},{6,4},{7,5},{8,10},{9,11},{10,... | collective-permute-start | bytes 147464 | tf_op jit(solution)/shard_map/ppermute | solution.py:155
  14.3 3.0 %copy-start.1 = (s32[192,1,4]{0,2,1:T(4,128)S(1)}, s32[192,1,4]{0,2,1:T(4,128)}, u32[]{:S(2)}) copy-start(s32[192,1,4]{0,2,1:T(4,128)} %param.6) | copy-start | bytes 9220
  14.3 3.0 %copy-start.2 = (s32[192]{0:T(256)S(1)}, s32[192]{0:T(256)}, u32[]{:S(2)}) copy-start(s32[192]{0:T(256)} %param.7) | copy-start | bytes 2308
  19.2 1.2 %collective-permute-start.7 = (f32[8,128]{1,0:T(8,128)S(1)}, f32[8,128]{1,0:T(8,128)S(1)}, u32[]{:S(2)}, u32[]{:S(2)}) collective-permute-start(f32[8,128]{1,0:T(8,128)S(1)} %get-tuple-element.27), channel_id=1, source_target_pairs={{0,8},{8,0},{16,24},{24,16},{1,9},{9,1},{17,25},{25,17},{2,10},{10... | collective-permute-start | bytes 12296 | tf_op jit(solution)/shard_map/ppermute | solution.py:179

commit v5 on v4

--- a/solution.py
+++ b/solution.py
@@ -18,7 +18,7 @@
 CORES = 2
 LINE_LANE = 96
 
-ORDER = (4, 6, 5, 7, 1, 3, 2)
+ORDER = (4, 1, 6, 5, 7, 3, 2)
 
 VMEM = pl.BlockSpec(memory_space=pltpu.VMEM)
 SMEM = pl.BlockSpec(memory_space=pltpu.SMEM)

time: 32.4 us -> 31.4 us (0.969)
  blocking collectives: 11.1 us -> 9.62 us
  waiting for transfers between devices: 1.66 us -> 2.13 us
    all_to_all x1, blocking collectives: 11.1 us -> 9.62 us  [body(): lax.all_to_all(parts.reshape(chips * count, 8, 128), ('tm', 'slab'), 0, 0...]
    ppermute x7, waiting for transfers between devices: 0.5 us -> 0.97 us  [body(): lax.ppermute(chunk, 'slab', [(i, i ^ partner) for i in range(count)])]
  transfers between devices with their start and end apart: 8 -> 8, of which waited for: 2 -> 3; matrix products, arithmetic and copies ran while one was open for 0% -> 0% of each run, Pallas kernels for 8% -> 8%
where the time goes in v5:
time: 31.4 us; the launch traced here: 31.2 us
  starting transfers between devices  12.4 us (39%)
  blocking collectives  9.62 us (31%)
  Pallas kernels  5.33 us (17%)
  waiting for transfers between devices  2.13 us (7%)
  local copies, waits for them, and re-layouts  1 us (3%)
  between operations  0.69 us (2%)
    ppermute x7, starting transfers between devices, body(): lax.ppermute(chunk, 'slab', [(i, i ^ partner) for i in range(count)])  12.4 us
    all_to_all x1, blocking collectives, body(): lax.all_to_all(parts.reshape(chips * count, 8, 128), ('tm', 'slab'), 0, 0...  9.62 us
    pallas_call x1, Pallas kernels, body(): pl.pallas_call(split_kernel, out_shape=(shape, shape), in_specs=[pl.Block...  2.5 us
    pallas_call x1, Pallas kernels, body(): pl.pallas_call(functools.partial(project_kernel, partners), out_shape=(pl...  1.82 us
    ppermute x1, waiting for transfers between devices, body(): line = lax.ppermute(line, 'tm', [(i, i ^ 1) for i in range(times)])  1.16 us
    unnamed x6, local copies, waits for them, and re-layouts  1 us
    ppermute x7, waiting for transfers between devices, body(): lax.ppermute(chunk, 'slab', [(i, i ^ partner) for i in range(count)])  0.97 us
    pallas_call x1, Pallas kernels, body(): pl.pallas_call(functools.partial(finish_kernel, count, factor), out_shape...  0.74 us
  transfers between devices with their start and end apart: 8, of which 3 were waited for; matrix products, arithmetic and copies ran while one was open for 0% of the time, Pallas kernels for 8%

profile of v5, /device:TPU:0, one launch (start us, length us, event | category | flops | bytes accessed | tf_op | source)
XLA Modules:
  0.0 31.2 jit_solution(3295894663809426902)
XLA Ops:
  0.6 0.0 copy-start
  0.6 1.0 %copy-done = f32[1,96,1024]{2,1,0:T(8,128)S(1)} copy-done((f32[1,96,1024]{2,1,0:T(8,128)S(1)}, f32[1,96,1024]{2,1,0:T(8,128)}, u32[]{:S(2)}) %copy-start) | copy-done | bytes 393240
  1.6 0.3 pack.1
  1.9 4.1 %collective-permute-start = (f32[96,128]{1,0:T(8,128)S(1)}, f32[96,128]{1,0:T(8,128)S(1)}, u32[]{:S(2)}, u32[]{:S(2)}) collective-permute-start(f32[96,128]{1,0:T(8,128)S(1)} %get-tuple-element.17), channel_id=1, source_target_pairs={{0,4},{1,5},{2,6},{3,7},{4,0},{5,1},{6,2},{7,3},{8,12},{9,13},{10,... | collective-permute-start | bytes 147464 | tf_op jit(solution)/shard_map/ppermute | solution.py:155
  6.0 1.5 %collective-permute-start.1 = (f32[96,128]{1,0:T(8,128)S(1)}, f32[96,128]{1,0:T(8,128)S(1)}, u32[]{:S(2)}, u32[]{:S(2)}) collective-permute-start(f32[96,128]{1,0:T(8,128)S(1)} %get-tuple-element.18), channel_id=1, source_target_pairs={{0,1},{1,0},{2,3},{3,2},{4,5},{5,4},{6,7},{7,6},{8,9},{9,8},{10,11... | collective-permute-start | bytes 147464 | tf_op jit(solution)/shard_map/ppermute | solution.py:155
  7.5 1.3 %collective-permute-start.2 = (f32[96,128]{1,0:T(8,128)S(1)}, f32[96,128]{1,0:T(8,128)S(1)}, u32[]{:S(2)}, u32[]{:S(2)}) collective-permute-start(f32[96,128]{1,0:T(8,128)S(1)} %get-tuple-element.19), channel_id=1, source_target_pairs={{0,6},{1,7},{2,4},{3,5},{4,2},{5,3},{6,0},{7,1},{8,14},{9,15},{10,... | collective-permute-start | bytes 147464 | tf_op jit(solution)/shard_map/ppermute | solution.py:155
  8.8 1.7 %collective-permute-start.3 = (f32[96,128]{1,0:T(8,128)S(1)}, f32[96,128]{1,0:T(8,128)S(1)}, u32[]{:S(2)}, u32[]{:S(2)}) collective-permute-start(f32[96,128]{1,0:T(8,128)S(1)} %get-tuple-element.20), channel_id=1, source_target_pairs={{0,5},{1,4},{2,7},{3,6},{4,1},{5,0},{6,3},{7,2},{8,13},{9,12},{10,... | collective-permute-start | bytes 147464 | tf_op jit(solution)/shard_map/ppermute | solution.py:155
  10.5 1.8 %collective-permute-start.4 = (f32[96,128]{1,0:T(8,128)S(1)}, f32[96,128]{1,0:T(8,128)S(1)}, u32[]{:S(2)}, u32[]{:S(2)}) collective-permute-start(f32[96,128]{1,0:T(8,128)S(1)} %get-tuple-element.21), channel_id=1, source_target_pairs={{0,7},{1,6},{2,5},{3,4},{4,3},{5,2},{6,1},{7,0},{8,15},{9,14},{10,... | collective-permute-start | bytes 147464 | tf_op jit(solution)/shard_map/ppermute | solution.py:155
  12.3 0.0 collective-permute-done.refs_1_
  12.3 0.9 %collective-permute-start.5 = (f32[96,128]{1,0:T(8,128)S(1)}, f32[96,128]{1,0:T(8,128)S(1)}, u32[]{:S(2)}, u32[]{:S(2)}) collective-permute-start(f32[96,128]{1,0:T(8,128)S(1)} %get-tuple-element.22), channel_id=1, source_target_pairs={{0,3},{1,2},{2,1},{3,0},{4,7},{5,6},{6,5},{7,4},{8,11},{9,10},{10,... | collective-permute-start | bytes 147464 | tf_op jit(solution)/shard_map/ppermute | solution.py:155
  13.2 0.0 collective-permute-done.1.refs_2_
  13.2 1.1 %collective-permute-start.6 = (f32[96,128]{1,0:T(8,128)S(1)}, f32[96,128]{1,0:T(8,128)S(1)}, u32[]{:S(2)}, u32[]{:S(2)}) collective-permute-start(f32[96,128]{1,0:T(8,128)S(1)} %get-tuple-element.23), channel_id=1, source_target_pairs={{0,2},{1,3},{2,0},{3,1},{4,6},{5,7},{6,4},{7,5},{8,10},{9,11},{10,... | collective-permute-start | bytes 147464 | tf_op jit(solution)/shard_map/ppermute | solution.py:155
  14.3 0.0 copy-start.1
  14.3 0.0 copy-start.2
  14.3 2.5 %split.1 = (bf16[1536,768]{1,0:T(8,128)(2,1)S(1)}, bf16[1536,768]{1,0:T(8,128)(2,1)S(1)}) custom-call(f32[2,3,192,1024]{3,2,1,0:T(8,128)} %bitcast.21), custom_call_target="tpu_custom_call" | custom-call | flops 7077888 | bytes 9437184 | tf_op jit(solution)/shard_map/split/pallas_call | solution.py:160
  16.8 0.0 collective-permute-done.2.refs_3_
  16.9 0.0 collective-permute-done.3.refs_4_
  16.9 0.8 %collective-permute-done.4.refs_5_ = f32[96,128]{1,0:T(8,128)S(1)} collective-permute-done((f32[96,128]{1,0:T(8,128)S(1)}, f32[96,128]{1,0:T(8,128)S(1)}, u32[]{:S(2)}, u32[]{:S(2)}) %collective-permute-start.4) | collective-permute-done | bytes 49184 | tf_op jit(solution)/shard_map/ppermute | solution.py:155
  17.7 0.2 collective-permute-done.5.refs_6_
  17.8 0.0 collective-permute-done.6.refs_7_
  17.8 0.0 copy-done.1
  17.8 0.0 copy-done.2
  17.8 1.8 %project.1 = (f32[8,8,128]{2,1,0:T(8,128)S(1)}, f32[8,128]{1,0:T(8,128)S(1)}) custom-call(s32[1]{0:T(128)} %bitcast.1.index_ref, f32[96,128]{1,0:T(8,128)S(1)} %get-tuple-element.16.refs_0_, f32[96,128]{1,0:T(8,128)S(1)} %collective-permute-done.refs_1_, f32[96,128]{1,0:T(8,128)S(1)} %collective-permute-done.1.refs_2_, ...), custom_call_target="tpu_custom_call" | custom-call | tf_op jit(solution)/shard_map/project/pallas_call | solution.py:170
  19.7 0.0 collective-permute-start.7
  19.7 1.2 %collective-permute-done.7.line_ref = f32[8,128]{1,0:T(8,128)S(1)} collective-permute-done((f32[8,128]{1,0:T(8,128)S(1)}, f32[8,128]{1,0:T(8,128)S(1)}, u32[]{:S(2)}, u32[]{:S(2)}) %collective-permute-start.7) | collective-permute-done | bytes 4128 | tf_op jit(solution)/shard_map/ppermute | solution.py:179
  20.8 9.6 %all_to_all.5 = f32[16,8,128]{2,1,0:T(8,128)S(1)} all-to-all(f32[16,8,128]{2,1,0:T(8,128)S(1)} %bitcast.18), channel_id=1, replica_groups={{23,22,21,20,19,18,17,16,7,6,5,4,3,2,1,0},{31,30,29,28,27,26,25,24,15,1..., dimensions={0} | all-to-all | bytes 131072 | tf_op jit(solution)/shard_map/all_to_all | solution.py:193
  30.5 0.7 %finish.1 = (f32[32,24]{1,0:T(8,128)}, f32[2,4,8]{2,1,0:T(4,128)}) custom-call(s32[1]{0:T(128)} %bitcast.time_ref.index_ref, f32[2,8,8,128]{3,2,1,0:T(8,128)S(1)} %bitcast.17), custom_call_target="tpu_custom_call" | custom-call | tf_op jit(solution)/shard_map/finish/pallas_call | solution.py:197
  (1 shorter events, 0.0 us)
Async XLA Ops:
  0.6 1.0 %copy-start = (f32[1,96,1024]{2,1,0:T(8,128)S(1)}, f32[1,96,1024]{2,1,0:T(8,128)}, u32[]{:S(2)}) copy-start(f32[1,96,1024]{2,1,0:T(8,128)} %param.4) | copy-start | bytes 1179652
  1.9 10.4 %collective-permute-start = (f32[96,128]{1,0:T(8,128)S(1)}, f32[96,128]{1,0:T(8,128)S(1)}, u32[]{:S(2)}, u32[]{:S(2)}) collective-permute-start(f32[96,128]{1,0:T(8,128)S(1)} %get-tuple-element.17), channel_id=1, source_target_pairs={{0,4},{1,5},{2,6},{3,7},{4,0},{5,1},{6,2},{7,3},{8,12},{9,13},{10,... | collective-permute-start | bytes 147464 | tf_op jit(solution)/shard_map/ppermute | solution.py:155
  6.0 7.2 %collective-permute-start.1 = (f32[96,128]{1,0:T(8,128)S(1)}, f32[96,128]{1,0:T(8,128)S(1)}, u32[]{:S(2)}, u32[]{:S(2)}) collective-permute-start(f32[96,128]{1,0:T(8,128)S(1)} %get-tuple-element.18), channel_id=1, source_target_pairs={{0,1},{1,0},{2,3},{3,2},{4,5},{5,4},{6,7},{7,6},{8,9},{9,8},{10,11... | collective-permute-start | bytes 147464 | tf_op jit(solution)/shard_map/ppermute | solution.py:155
  7.5 9.4 %collective-permute-start.2 = (f32[96,128]{1,0:T(8,128)S(1)}, f32[96,128]{1,0:T(8,128)S(1)}, u32[]{:S(2)}, u32[]{:S(2)}) collective-permute-start(f32[96,128]{1,0:T(8,128)S(1)} %get-tuple-element.19), channel_id=1, source_target_pairs={{0,6},{1,7},{2,4},{3,5},{4,2},{5,3},{6,0},{7,1},{8,14},{9,15},{10,... | collective-permute-start | bytes 147464 | tf_op jit(solution)/shard_map/ppermute | solution.py:155
  8.8 8.0 %collective-permute-start.3 = (f32[96,128]{1,0:T(8,128)S(1)}, f32[96,128]{1,0:T(8,128)S(1)}, u32[]{:S(2)}, u32[]{:S(2)}) collective-permute-start(f32[96,128]{1,0:T(8,128)S(1)} %get-tuple-element.20), channel_id=1, source_target_pairs={{0,5},{1,4},{2,7},{3,6},{4,1},{5,0},{6,3},{7,2},{8,13},{9,12},{10,... | collective-permute-start | bytes 147464 | tf_op jit(solution)/shard_map/ppermute | solution.py:155
  10.5 7.2 %collective-permute-start.4 = (f32[96,128]{1,0:T(8,128)S(1)}, f32[96,128]{1,0:T(8,128)S(1)}, u32[]{:S(2)}, u32[]{:S(2)}) collective-permute-start(f32[96,128]{1,0:T(8,128)S(1)} %get-tuple-element.21), channel_id=1, source_target_pairs={{0,7},{1,6},{2,5},{3,4},{4,3},{5,2},{6,1},{7,0},{8,15},{9,14},{10,... | collective-permute-start | bytes 147464 | tf_op jit(solution)/shard_map/ppermute | solution.py:155
  12.3 5.5 %collective-permute-start.5 = (f32[96,128]{1,0:T(8,128)S(1)}, f32[96,128]{1,0:T(8,128)S(1)}, u32[]{:S(2)}, u32[]{:S(2)}) collective-permute-start(f32[96,128]{1,0:T(8,128)S(1)} %get-tuple-element.22), channel_id=1, source_target_pairs={{0,3},{1,2},{2,1},{3,0},{4,7},{5,6},{6,5},{7,4},{8,11},{9,10},{10,... | collective-permute-start | bytes 147464 | tf_op jit(solution)/shard_map/ppermute | solution.py:155
  13.2 4.6 %collective-permute-start.6 = (f32[96,128]{1,0:T(8,128)S(1)}, f32[96,128]{1,0:T(8,128)S(1)}, u32[]{:S(2)}, u32[]{:S(2)}) collective-permute-start(f32[96,128]{1,0:T(8,128)S(1)} %get-tuple-element.23), channel_id=1, source_target_pairs={{0,2},{1,3},{2,0},{3,1},{4,6},{5,7},{6,4},{7,5},{8,10},{9,11},{10,... | collective-permute-start | bytes 147464 | tf_op jit(solution)/shard_map/ppermute | solution.py:155
  14.3 3.5 %copy-start.1 = (s32[192,1,4]{0,2,1:T(4,128)S(1)}, s32[192,1,4]{0,2,1:T(4,128)}, u32[]{:S(2)}) copy-start(s32[192,1,4]{0,2,1:T(4,128)} %param.6) | copy-start | bytes 9220
  14.3 3.5 %copy-start.2 = (s32[192]{0:T(256)S(1)}, s32[192]{0:T(256)}, u32[]{:S(2)}) copy-start(s32[192]{0:T(256)} %param.7) | copy-start | bytes 2308
  19.7 1.2 %collective-permute-start.7 = (f32[8,128]{1,0:T(8,128)S(1)}, f32[8,128]{1,0:T(8,128)S(1)}, u32[]{:S(2)}, u32[]{:S(2)}) collective-permute-start(f32[8,128]{1,0:T(8,128)S(1)} %get-tuple-element.27), channel_id=1, source_target_pairs={{0,8},{8,0},{16,24},{24,16},{1,9},{9,1},{17,25},{25,17},{2,10},{10... | collective-permute-start | bytes 12296 | tf_op jit(solution)/shard_map/ppermute | solution.py:179

commit v6 on v5

--- a/solution.py
+++ b/solution.py
@@ -18,7 +18,7 @@
 CORES = 2
 LINE_LANE = 96
 
-ORDER = (4, 1, 6, 5, 7, 3, 2)
+ORDER = (4, 3, 6, 5, 7, 2, 1)
 
 VMEM = pl.BlockSpec(memory_space=pltpu.VMEM)
 SMEM = pl.BlockSpec(memory_space=pltpu.SMEM)

time: 31.4 us -> 31.3 us (level)
  no operation moved by 1% of the time
where the time goes in v6:
time: 31.3 us; the launch traced here: 31.1 us
  starting transfers between devices  12.5 us (40%)
  blocking collectives  9.63 us (31%)
  Pallas kernels  5.32 us (17%)
  waiting for transfers between devices  1.98 us (6%)
  local copies, waits for them, and re-layouts  1 us (3%)
  between operations  0.69 us (2%)
    ppermute x7, starting transfers between devices, body(): lax.ppermute(chunk, 'slab', [(i, i ^ partner) for i in range(count)])  12.5 us
    all_to_all x1, blocking collectives, body(): lax.all_to_all(parts.reshape(chips * count, 8, 128), ('tm', 'slab'), 0, 0...  9.63 us
    pallas_call x1, Pallas kernels, body(): pl.pallas_call(split_kernel, out_shape=(shape, shape), in_specs=[pl.Block...  2.5 us
    pallas_call x1, Pallas kernels, body(): pl.pallas_call(functools.partial(project_kernel, partners), out_shape=(pl...  1.81 us
    ppermute x1, waiting for transfers between devices, body(): line = lax.ppermute(line, 'tm', [(i, i ^ 1) for i in range(times)])  1.16 us
    unnamed x6, local copies, waits for them, and re-layouts  1 us
    ppermute x7, waiting for transfers between devices, body(): lax.ppermute(chunk, 'slab', [(i, i ^ partner) for i in range(count)])  0.82 us
    pallas_call x1, Pallas kernels, body(): pl.pallas_call(functools.partial(finish_kernel, count, factor), out_shape...  0.74 us
  transfers between devices with their start and end apart: 8, of which 3 were waited for; matrix products, arithmetic and copies ran while one was open for 0% of the time, Pallas kernels for 8%

profile of v6, /device:TPU:0, one launch (start us, length us, event | category | flops | bytes accessed | tf_op | source)
XLA Modules:
  0.0 31.1 jit_solution(4652800708963355947)
XLA Ops:
  0.6 0.0 copy-start
  0.6 1.0 %copy-done = f32[1,96,1024]{2,1,0:T(8,128)S(1)} copy-done((f32[1,96,1024]{2,1,0:T(8,128)S(1)}, f32[1,96,1024]{2,1,0:T(8,128)}, u32[]{:S(2)}) %copy-start) | copy-done | bytes 393240
  1.6 0.3 pack.1
  1.9 4.1 %collective-permute-start = (f32[96,128]{1,0:T(8,128)S(1)}, f32[96,128]{1,0:T(8,128)S(1)}, u32[]{:S(2)}, u32[]{:S(2)}) collective-permute-start(f32[96,128]{1,0:T(8,128)S(1)} %get-tuple-element.17), channel_id=1, source_target_pairs={{0,4},{1,5},{2,6},{3,7},{4,0},{5,1},{6,2},{7,3},{8,12},{9,13},{10,... | collective-permute-start | bytes 147464 | tf_op jit(solution)/shard_map/ppermute | solution.py:155
  6.0 2.5 %collective-permute-start.1 = (f32[96,128]{1,0:T(8,128)S(1)}, f32[96,128]{1,0:T(8,128)S(1)}, u32[]{:S(2)}, u32[]{:S(2)}) collective-permute-start(f32[96,128]{1,0:T(8,128)S(1)} %get-tuple-element.18), channel_id=1, source_target_pairs={{0,3},{1,2},{2,1},{3,0},{4,7},{5,6},{6,5},{7,4},{8,11},{9,10},{10,... | collective-permute-start | bytes 147464 | tf_op jit(solution)/shard_map/ppermute | solution.py:155
  8.5 0.2 collective-permute-start.2
  8.7 1.7 %collective-permute-start.3 = (f32[96,128]{1,0:T(8,128)S(1)}, f32[96,128]{1,0:T(8,128)S(1)}, u32[]{:S(2)}, u32[]{:S(2)}) collective-permute-start(f32[96,128]{1,0:T(8,128)S(1)} %get-tuple-element.20), channel_id=1, source_target_pairs={{0,5},{1,4},{2,7},{3,6},{4,1},{5,0},{6,3},{7,2},{8,13},{9,12},{10,... | collective-permute-start | bytes 147464 | tf_op jit(solution)/shard_map/ppermute | solution.py:155
  10.4 2.3 %collective-permute-start.4 = (f32[96,128]{1,0:T(8,128)S(1)}, f32[96,128]{1,0:T(8,128)S(1)}, u32[]{:S(2)}, u32[]{:S(2)}) collective-permute-start(f32[96,128]{1,0:T(8,128)S(1)} %get-tuple-element.21), channel_id=1, source_target_pairs={{0,7},{1,6},{2,5},{3,4},{4,3},{5,2},{6,1},{7,0},{8,15},{9,14},{10,... | collective-permute-start | bytes 147464 | tf_op jit(solution)/shard_map/ppermute | solution.py:155
  12.7 0.0 collective-permute-done.refs_1_
  12.7 0.5 %collective-permute-start.5 = (f32[96,128]{1,0:T(8,128)S(1)}, f32[96,128]{1,0:T(8,128)S(1)}, u32[]{:S(2)}, u32[]{:S(2)}) collective-permute-start(f32[96,128]{1,0:T(8,128)S(1)} %get-tuple-element.22), channel_id=1, source_target_pairs={{0,2},{1,3},{2,0},{3,1},{4,6},{5,7},{6,4},{7,5},{8,10},{9,11},{10,... | collective-permute-start | bytes 147464 | tf_op jit(solution)/shard_map/ppermute | solution.py:155
  13.1 0.0 collective-permute-done.1.refs_2_
  13.1 1.2 %collective-permute-start.6 = (f32[96,128]{1,0:T(8,128)S(1)}, f32[96,128]{1,0:T(8,128)S(1)}, u32[]{:S(2)}, u32[]{:S(2)}) collective-permute-start(f32[96,128]{1,0:T(8,128)S(1)} %get-tuple-element.23), channel_id=1, source_target_pairs={{0,1},{1,0},{2,3},{3,2},{4,5},{5,4},{6,7},{7,6},{8,9},{9,8},{10,11... | collective-permute-start | bytes 147464 | tf_op jit(solution)/shard_map/ppermute | solution.py:155
  14.4 0.0 copy-start.1
  14.4 0.0 copy-start.2
  14.4 2.5 %split.1 = (bf16[1536,768]{1,0:T(8,128)(2,1)S(1)}, bf16[1536,768]{1,0:T(8,128)(2,1)S(1)}) custom-call(f32[2,3,192,1024]{3,2,1,0:T(8,128)} %bitcast.21), custom_call_target="tpu_custom_call" | custom-call | flops 7077888 | bytes 9437184 | tf_op jit(solution)/shard_map/split/pallas_call | solution.py:160
  16.9 0.0 collective-permute-done.2.refs_3_
  16.9 0.0 collective-permute-done.3.refs_4_
  16.9 0.3 %collective-permute-done.4.refs_5_ = f32[96,128]{1,0:T(8,128)S(1)} collective-permute-done((f32[96,128]{1,0:T(8,128)S(1)}, f32[96,128]{1,0:T(8,128)S(1)}, u32[]{:S(2)}, u32[]{:S(2)}) %collective-permute-start.4) | collective-permute-done | bytes 49184 | tf_op jit(solution)/shard_map/ppermute | solution.py:155
  17.2 0.0 collective-permute-done.5.refs_6_
  17.2 0.5 %collective-permute-done.6.refs_7_ = f32[96,128]{1,0:T(8,128)S(1)} collective-permute-done((f32[96,128]{1,0:T(8,128)S(1)}, f32[96,128]{1,0:T(8,128)S(1)}, u32[]{:S(2)}, u32[]{:S(2)}) %collective-permute-start.6) | collective-permute-done | bytes 49184 | tf_op jit(solution)/shard_map/ppermute | solution.py:155
  17.7 0.0 copy-done.1
  17.7 0.0 copy-done.2
  17.7 1.8 %project.1 = (f32[8,8,128]{2,1,0:T(8,128)S(1)}, f32[8,128]{1,0:T(8,128)S(1)}) custom-call(s32[1]{0:T(128)} %bitcast.1.index_ref, f32[96,128]{1,0:T(8,128)S(1)} %get-tuple-element.16.refs_0_, f32[96,128]{1,0:T(8,128)S(1)} %collective-permute-done.refs_1_, f32[96,128]{1,0:T(8,128)S(1)} %collective-permute-done.1.refs_2_, ...), custom_call_target="tpu_custom_call" | custom-call | tf_op jit(solution)/shard_map/project/pallas_call | solution.py:170
  19.5 0.0 collective-permute-start.7
  19.5 1.2 %collective-permute-done.7.line_ref = f32[8,128]{1,0:T(8,128)S(1)} collective-permute-done((f32[8,128]{1,0:T(8,128)S(1)}, f32[8,128]{1,0:T(8,128)S(1)}, u32[]{:S(2)}, u32[]{:S(2)}) %collective-permute-start.7) | collective-permute-done | bytes 4128 | tf_op jit(solution)/shard_map/ppermute | solution.py:179
  20.7 9.6 %all_to_all.5 = f32[16,8,128]{2,1,0:T(8,128)S(1)} all-to-all(f32[16,8,128]{2,1,0:T(8,128)S(1)} %bitcast.18), channel_id=1, replica_groups={{23,22,21,20,19,18,17,16,7,6,5,4,3,2,1,0},{31,30,29,28,27,26,25,24,15,1..., dimensions={0} | all-to-all | bytes 131072 | tf_op jit(solution)/shard_map/all_to_all | solution.py:193
  30.4 0.7 %finish.1 = (f32[32,24]{1,0:T(8,128)}, f32[2,4,8]{2,1,0:T(4,128)}) custom-call(s32[1]{0:T(128)} %bitcast.time_ref.index_ref, f32[2,8,8,128]{3,2,1,0:T(8,128)S(1)} %bitcast.17), custom_call_target="tpu_custom_call" | custom-call | tf_op jit(solution)/shard_map/finish/pallas_call | solution.py:197
  (1 shorter events, 0.0 us)
Async XLA Ops:
  0.6 1.0 %copy-start = (f32[1,96,1024]{2,1,0:T(8,128)S(1)}, f32[1,96,1024]{2,1,0:T(8,128)}, u32[]{:S(2)}) copy-start(f32[1,96,1024]{2,1,0:T(8,128)} %param.4) | copy-start | bytes 1179652
  1.9 10.8 %collective-permute-start = (f32[96,128]{1,0:T(8,128)S(1)}, f32[96,128]{1,0:T(8,128)S(1)}, u32[]{:S(2)}, u32[]{:S(2)}) collective-permute-start(f32[96,128]{1,0:T(8,128)S(1)} %get-tuple-element.17), channel_id=1, source_target_pairs={{0,4},{1,5},{2,6},{3,7},{4,0},{5,1},{6,2},{7,3},{8,12},{9,13},{10,... | collective-permute-start | bytes 147464 | tf_op jit(solution)/shard_map/ppermute | solution.py:155
  6.0 7.1 %collective-permute-start.1 = (f32[96,128]{1,0:T(8,128)S(1)}, f32[96,128]{1,0:T(8,128)S(1)}, u32[]{:S(2)}, u32[]{:S(2)}) collective-permute-start(f32[96,128]{1,0:T(8,128)S(1)} %get-tuple-element.18), channel_id=1, source_target_pairs={{0,3},{1,2},{2,1},{3,0},{4,7},{5,6},{6,5},{7,4},{8,11},{9,10},{10,... | collective-permute-start | bytes 147464 | tf_op jit(solution)/shard_map/ppermute | solution.py:155
  8.5 8.4 %collective-permute-start.2 = (f32[96,128]{1,0:T(8,128)S(1)}, f32[96,128]{1,0:T(8,128)S(1)}, u32[]{:S(2)}, u32[]{:S(2)}) collective-permute-start(f32[96,128]{1,0:T(8,128)S(1)} %get-tuple-element.19), channel_id=1, source_target_pairs={{0,6},{1,7},{2,4},{3,5},{4,2},{5,3},{6,0},{7,1},{8,14},{9,15},{10,... | collective-permute-start | bytes 147464 | tf_op jit(solution)/shard_map/ppermute | solution.py:155
  8.7 8.2 %collective-permute-start.3 = (f32[96,128]{1,0:T(8,128)S(1)}, f32[96,128]{1,0:T(8,128)S(1)}, u32[]{:S(2)}, u32[]{:S(2)}) collective-permute-start(f32[96,128]{1,0:T(8,128)S(1)} %get-tuple-element.20), channel_id=1, source_target_pairs={{0,5},{1,4},{2,7},{3,6},{4,1},{5,0},{6,3},{7,2},{8,13},{9,12},{10,... | collective-permute-start | bytes 147464 | tf_op jit(solution)/shard_map/ppermute | solution.py:155
  10.4 6.9 %collective-permute-start.4 = (f32[96,128]{1,0:T(8,128)S(1)}, f32[96,128]{1,0:T(8,128)S(1)}, u32[]{:S(2)}, u32[]{:S(2)}) collective-permute-start(f32[96,128]{1,0:T(8,128)S(1)} %get-tuple-element.21), channel_id=1, source_target_pairs={{0,7},{1,6},{2,5},{3,4},{4,3},{5,2},{6,1},{7,0},{8,15},{9,14},{10,... | collective-permute-start | bytes 147464 | tf_op jit(solution)/shard_map/ppermute | solution.py:155
  12.7 4.6 %collective-permute-start.5 = (f32[96,128]{1,0:T(8,128)S(1)}, f32[96,128]{1,0:T(8,128)S(1)}, u32[]{:S(2)}, u32[]{:S(2)}) collective-permute-start(f32[96,128]{1,0:T(8,128)S(1)} %get-tuple-element.22), channel_id=1, source_target_pairs={{0,2},{1,3},{2,0},{3,1},{4,6},{5,7},{6,4},{7,5},{8,10},{9,11},{10,... | collective-permute-start | bytes 147464 | tf_op jit(solution)/shard_map/ppermute | solution.py:155
  13.1 4.6 %collective-permute-start.6 = (f32[96,128]{1,0:T(8,128)S(1)}, f32[96,128]{1,0:T(8,128)S(1)}, u32[]{:S(2)}, u32[]{:S(2)}) collective-permute-start(f32[96,128]{1,0:T(8,128)S(1)} %get-tuple-element.23), channel_id=1, source_target_pairs={{0,1},{1,0},{2,3},{3,2},{4,5},{5,4},{6,7},{7,6},{8,9},{9,8},{10,11... | collective-permute-start | bytes 147464 | tf_op jit(solution)/shard_map/ppermute | solution.py:155
  14.4 3.4 %copy-start.1 = (s32[192,1,4]{0,2,1:T(4,128)S(1)}, s32[192,1,4]{0,2,1:T(4,128)}, u32[]{:S(2)}) copy-start(s32[192,1,4]{0,2,1:T(4,128)} %param.6) | copy-start | bytes 9220
  14.4 3.4 %copy-start.2 = (s32[192]{0:T(256)S(1)}, s32[192]{0:T(256)}, u32[]{:S(2)}) copy-start(s32[192]{0:T(256)} %param.7) | copy-start | bytes 2308
  19.5 1.2 %collective-permute-start.7 = (f32[8,128]{1,0:T(8,128)S(1)}, f32[8,128]{1,0:T(8,128)S(1)}, u32[]{:S(2)}, u32[]{:S(2)}) collective-permute-start(f32[8,128]{1,0:T(8,128)S(1)} %get-tuple-element.27), channel_id=1, source_target_pairs={{0,8},{8,0},{16,24},{24,16},{1,9},{9,1},{17,25},{25,17},{2,10},{10... | collective-permute-start | bytes 12296 | tf_op jit(solution)/shard_map/ppermute | solution.py:179

commit v7 on v6

--- a/solution.py
+++ b/solution.py
@@ -58,21 +58,22 @@
     ]
     for copy in copies:
         copy.start()
-    for copy, (part, color) in zip(copies, steps):
-        copy.wait()
+    for color in range(NCOLOR):
+        for copy in copies[2 * color : 2 * color + 2]:
+            copy.wait()
         for g in range(GROUPS):
-            rows = pl.ds((g * 2 + part) * NEIG, NEIG)
-            lanes = pl.ds(color * width, width)
-            high, low = split(landed[part, color, :, pl.ds(g * width, width)])
-            high_ref[rows, lanes] = high
-            low_ref[rows, lanes] = low
+            rows = pl.ds((g * NCOLOR + color) * width, width)
+            both = jnp.concatenate([landed[part, color, :, pl.ds(g * width, width)] for part in range(2)], axis=0)
+            high, low = split(both.T)
+            high_ref[rows, :] = high
+            low_ref[rows, :] = low
 
 
 def project_kernel(partners, index_ref, *refs):
     count = len(partners)
     field_refs = refs[:count]
     high_ref, low_ref, noise_ref, block_ref, out_ref, line_ref, weights = refs[count:]
-    width = high_ref.shape[1] // NCOLOR
+    width = high_ref.shape[0] // (GROUPS * NCOLOR)
     rows = width // count
     per = NEIG // count
     for partner, field_ref in zip(partners, field_refs):
@@ -83,10 +84,10 @@
     dims = (((1,), (1,)), ((), ()))
     total = jnp.zeros((COLS, 2 * NEIG), jnp.float32)
     for g in range(GROUPS):
-        vecs, columns = pl.ds(g * 2 * NEIG, 2 * NEIG), slice(g * COLS, (g + 1) * COLS)
+        vecs, columns = pl.ds(g * NCOLOR * width, NCOLOR * width), slice(g * COLS, (g + 1) * COLS)
         both = jnp.concatenate([high[columns], low[columns]], axis=0)
-        first = lax.dot_general(both, high_ref[vecs, :], dims, preferred_element_type=jnp.float32)
-        second = lax.dot_general(high[columns], low_ref[vecs, :], dims, preferred_element_type=jnp.float32)
+        first = jnp.dot(both, high_ref[vecs, :], preferred_element_type=jnp.float32)
+        second = jnp.dot(high[columns], low_ref[vecs, :], preferred_element_type=jnp.float32)
         total += first[:COLS] + (first[COLS:] + second)
     with_real, with_imag = total[:, :NEIG], total[:, NEIG:]
     real = with_real[:PAIRS] + with_imag[PAIRS:]
@@ -156,7 +157,7 @@
         for partner, chunk in zip(partners, chunks)
     ]
     vectors = jnp.transpose(eigvecs.reshape(eigvecs.shape[1:]), (0, 2, 1, 3))
-    shape = jax.ShapeDtypeStruct((2 * GROUPS * NEIG, NCOLOR * sites // GROUPS), jnp.bfloat16)
+    shape = jax.ShapeDtypeStruct((NCOLOR * sites, 2 * NEIG), jnp.bfloat16)
     high, low = pl.pallas_call(
         split_kernel,
         out_shape=(shape, shape),

time: 31.3 us -> 30.8 us (0.984)
  waiting for transfers between devices: 1.98 us -> 1.59 us
    pallas_call x1, Pallas kernels: 1.81 us -> 1.22 us  [body(): pl.pallas_call(functools.partial(project_kernel, partners), out_shape=(pl...]
    ppermute x7, waiting for transfers between devices: 0.82 us -> 0.43 us  [body(): lax.ppermute(chunk, 'slab', [(i, i ^ partner) for i in range(count)])]
    pallas_call x1, Pallas kernels: 2.5 us -> 2.88 us  [body(): pl.pallas_call(split_kernel, out_shape=(shape, shape), in_specs=[pl.Block...]
  transfers between devices with their start and end apart: 8 -> 8, of which waited for: 3 -> 2; matrix products, arithmetic and copies ran while one was open for 0% -> 0% of each run, Pallas kernels for 8% -> 9%
where the time goes in v7:
time: 30.8 us; the launch traced here: 30.6 us
  starting transfers between devices  12.5 us (41%)
  blocking collectives  9.71 us (32%)
  Pallas kernels  5.1 us (17%)
  waiting for transfers between devices  1.59 us (5%)
  local copies, waits for them, and re-layouts  1 us (3%)
  between operations  0.71 us (2%)
    ppermute x7, starting transfers between devices, body(): lax.ppermute(chunk, 'slab', [(i, i ^ partner) for i in range(count)])  12.5 us
    all_to_all x1, blocking collectives, body(): lax.all_to_all(parts.reshape(chips * count, 8, 128), ('tm', 'slab'), 0, 0...  9.71 us
    pallas_call x1, Pallas kernels, body(): pl.pallas_call(split_kernel, out_shape=(shape, shape), in_specs=[pl.Block...  2.88 us
    pallas_call x1, Pallas kernels, body(): pl.pallas_call(functools.partial(project_kernel, partners), out_shape=(pl...  1.22 us
    ppermute x1, waiting for transfers between devices, body(): line = lax.ppermute(line, 'tm', [(i, i ^ 1) for i in range(times)])  1.16 us
    unnamed x6, local copies, waits for them, and re-layouts  1 us
    pallas_call x1, Pallas kernels, body(): pl.pallas_call(functools.partial(finish_kernel, count, factor), out_shape...  0.74 us
  transfers between devices with their start and end apart: 8, of which 2 were waited for; matrix products, arithmetic and copies ran while one was open for 0% of the time, Pallas kernels for 9%

profile of v7, /device:TPU:0, one launch (start us, length us, event | category | flops | bytes accessed | tf_op | source)
XLA Modules:
  0.0 30.6 jit_solution(6872934619241824606)
XLA Ops:
  0.6 0.0 copy-start
  0.6 1.0 %copy-done = f32[1,96,1024]{2,1,0:T(8,128)S(1)} copy-done((f32[1,96,1024]{2,1,0:T(8,128)S(1)}, f32[1,96,1024]{2,1,0:T(8,128)}, u32[]{:S(2)}) %copy-start) | copy-done | bytes 393240
  1.6 0.3 pack.1
  1.9 4.1 %collective-permute-start = (f32[96,128]{1,0:T(8,128)S(1)}, f32[96,128]{1,0:T(8,128)S(1)}, u32[]{:S(2)}, u32[]{:S(2)}) collective-permute-start(f32[96,128]{1,0:T(8,128)S(1)} %get-tuple-element.17), channel_id=1, source_target_pairs={{0,4},{1,5},{2,6},{3,7},{4,0},{5,1},{6,2},{7,3},{8,12},{9,13},{10,... | collective-permute-start | bytes 147464 | tf_op jit(solution)/shard_map/ppermute | solution.py:156
  6.0 2.5 %collective-permute-start.1 = (f32[96,128]{1,0:T(8,128)S(1)}, f32[96,128]{1,0:T(8,128)S(1)}, u32[]{:S(2)}, u32[]{:S(2)}) collective-permute-start(f32[96,128]{1,0:T(8,128)S(1)} %get-tuple-element.18), channel_id=1, source_target_pairs={{0,3},{1,2},{2,1},{3,0},{4,7},{5,6},{6,5},{7,4},{8,11},{9,10},{10,... | collective-permute-start | bytes 147464 | tf_op jit(solution)/shard_map/ppermute | solution.py:156
  8.5 0.2 collective-permute-start.2
  8.7 1.7 %collective-permute-start.3 = (f32[96,128]{1,0:T(8,128)S(1)}, f32[96,128]{1,0:T(8,128)S(1)}, u32[]{:S(2)}, u32[]{:S(2)}) collective-permute-start(f32[96,128]{1,0:T(8,128)S(1)} %get-tuple-element.20), channel_id=1, source_target_pairs={{0,5},{1,4},{2,7},{3,6},{4,1},{5,0},{6,3},{7,2},{8,13},{9,12},{10,... | collective-permute-start | bytes 147464 | tf_op jit(solution)/shard_map/ppermute | solution.py:156
  10.4 2.3 %collective-permute-start.4 = (f32[96,128]{1,0:T(8,128)S(1)}, f32[96,128]{1,0:T(8,128)S(1)}, u32[]{:S(2)}, u32[]{:S(2)}) collective-permute-start(f32[96,128]{1,0:T(8,128)S(1)} %get-tuple-element.21), channel_id=1, source_target_pairs={{0,7},{1,6},{2,5},{3,4},{4,3},{5,2},{6,1},{7,0},{8,15},{9,14},{10,... | collective-permute-start | bytes 147464 | tf_op jit(solution)/shard_map/ppermute | solution.py:156
  12.7 0.0 collective-permute-done.refs_1_
  12.7 0.5 %collective-permute-start.5 = (f32[96,128]{1,0:T(8,128)S(1)}, f32[96,128]{1,0:T(8,128)S(1)}, u32[]{:S(2)}, u32[]{:S(2)}) collective-permute-start(f32[96,128]{1,0:T(8,128)S(1)} %get-tuple-element.22), channel_id=1, source_target_pairs={{0,2},{1,3},{2,0},{3,1},{4,6},{5,7},{6,4},{7,5},{8,10},{9,11},{10,... | collective-permute-start | bytes 147464 | tf_op jit(solution)/shard_map/ppermute | solution.py:156
  13.1 0.0 collective-permute-done.1.refs_2_
  13.1 1.2 %collective-permute-start.6 = (f32[96,128]{1,0:T(8,128)S(1)}, f32[96,128]{1,0:T(8,128)S(1)}, u32[]{:S(2)}, u32[]{:S(2)}) collective-permute-start(f32[96,128]{1,0:T(8,128)S(1)} %get-tuple-element.23), channel_id=1, source_target_pairs={{0,1},{1,0},{2,3},{3,2},{4,5},{5,4},{6,7},{7,6},{8,9},{9,8},{10,11... | collective-permute-start | bytes 147464 | tf_op jit(solution)/shard_map/ppermute | solution.py:156
  14.4 0.0 copy-start.1
  14.4 0.0 copy-start.2
  14.4 2.9 %split.1 = (bf16[3072,384]{1,0:T(8,128)(2,1)S(1)}, bf16[3072,384]{1,0:T(8,128)(2,1)S(1)}) custom-call(f32[2,3,192,1024]{3,2,1,0:T(8,128)} %bitcast.21), custom_call_target="tpu_custom_call" | custom-call | flops 7077888 | bytes 9437184 | tf_op jit(solution)/shard_map/split/pallas_call | solution.py:161
  17.3 0.0 collective-permute-done.2.refs_3_
  17.3 0.0 collective-permute-done.3.refs_4_
  17.3 0.0 collective-permute-done.4.refs_5_
  17.3 0.0 collective-permute-done.5.refs_6_
  17.3 0.4 %collective-permute-done.6.refs_7_ = f32[96,128]{1,0:T(8,128)S(1)} collective-permute-done((f32[96,128]{1,0:T(8,128)S(1)}, f32[96,128]{1,0:T(8,128)S(1)}, u32[]{:S(2)}, u32[]{:S(2)}) %collective-permute-start.6) | collective-permute-done | bytes 49184 | tf_op jit(solution)/shard_map/ppermute | solution.py:156
  17.7 0.0 copy-done.1
  17.7 0.0 copy-done.2
  17.7 1.2 %project.1 = (f32[8,8,128]{2,1,0:T(8,128)S(1)}, f32[8,128]{1,0:T(8,128)S(1)}) custom-call(s32[1]{0:T(128)} %bitcast.1.index_ref, f32[96,128]{1,0:T(8,128)S(1)} %get-tuple-element.16.refs_0_, f32[96,128]{1,0:T(8,128)S(1)} %collective-permute-done.refs_1_, f32[96,128]{1,0:T(8,128)S(1)} %collective-permute-done.1.refs_2_, ...), custom_call_target="tpu_custom_call" | custom-call | tf_op jit(solution)/shard_map/project/pallas_call | solution.py:171
  18.9 0.0 collective-permute-start.7
  19.0 1.2 %collective-permute-done.7.line_ref = f32[8,128]{1,0:T(8,128)S(1)} collective-permute-done((f32[8,128]{1,0:T(8,128)S(1)}, f32[8,128]{1,0:T(8,128)S(1)}, u32[]{:S(2)}, u32[]{:S(2)}) %collective-permute-start.7) | collective-permute-done | bytes 4128 | tf_op jit(solution)/shard_map/ppermute | solution.py:180
  20.1 9.7 %all_to_all.5 = f32[16,8,128]{2,1,0:T(8,128)S(1)} all-to-all(f32[16,8,128]{2,1,0:T(8,128)S(1)} %bitcast.18), channel_id=1, replica_groups={{23,22,21,20,19,18,17,16,7,6,5,4,3,2,1,0},{31,30,29,28,27,26,25,24,15,1..., dimensions={0} | all-to-all | bytes 131072 | tf_op jit(solution)/shard_map/all_to_all | solution.py:194
  29.8 0.7 %finish.1 = (f32[32,24]{1,0:T(8,128)}, f32[2,4,8]{2,1,0:T(4,128)}) custom-call(s32[1]{0:T(128)} %bitcast.time_ref.index_ref, f32[2,8,8,128]{3,2,1,0:T(8,128)S(1)} %bitcast.17), custom_call_target="tpu_custom_call" | custom-call | tf_op jit(solution)/shard_map/finish/pallas_call | solution.py:198
  (1 shorter events, 0.0 us)
Async XLA Ops:
  0.6 1.0 %copy-start = (f32[1,96,1024]{2,1,0:T(8,128)S(1)}, f32[1,96,1024]{2,1,0:T(8,128)}, u32[]{:S(2)}) copy-start(f32[1,96,1024]{2,1,0:T(8,128)} %param.4) | copy-start | bytes 1179652
  1.9 10.8 %collective-permute-start = (f32[96,128]{1,0:T(8,128)S(1)}, f32[96,128]{1,0:T(8,128)S(1)}, u32[]{:S(2)}, u32[]{:S(2)}) collective-permute-start(f32[96,128]{1,0:T(8,128)S(1)} %get-tuple-element.17), channel_id=1, source_target_pairs={{0,4},{1,5},{2,6},{3,7},{4,0},{5,1},{6,2},{7,3},{8,12},{9,13},{10,... | collective-permute-start | bytes 147464 | tf_op jit(solution)/shard_map/ppermute | solution.py:156
  6.0 7.1 %collective-permute-start.1 = (f32[96,128]{1,0:T(8,128)S(1)}, f32[96,128]{1,0:T(8,128)S(1)}, u32[]{:S(2)}, u32[]{:S(2)}) collective-permute-start(f32[96,128]{1,0:T(8,128)S(1)} %get-tuple-element.18), channel_id=1, source_target_pairs={{0,3},{1,2},{2,1},{3,0},{4,7},{5,6},{6,5},{7,4},{8,11},{9,10},{10,... | collective-permute-start | bytes 147464 | tf_op jit(solution)/shard_map/ppermute | solution.py:156
  8.5 8.8 %collective-permute-start.2 = (f32[96,128]{1,0:T(8,128)S(1)}, f32[96,128]{1,0:T(8,128)S(1)}, u32[]{:S(2)}, u32[]{:S(2)}) collective-permute-start(f32[96,128]{1,0:T(8,128)S(1)} %get-tuple-element.19), channel_id=1, source_target_pairs={{0,6},{1,7},{2,4},{3,5},{4,2},{5,3},{6,0},{7,1},{8,14},{9,15},{10,... | collective-permute-start | bytes 147464 | tf_op jit(solution)/shard_map/ppermute | solution.py:156
  8.7 8.5 %collective-permute-start.3 = (f32[96,128]{1,0:T(8,128)S(1)}, f32[96,128]{1,0:T(8,128)S(1)}, u32[]{:S(2)}, u32[]{:S(2)}) collective-permute-start(f32[96,128]{1,0:T(8,128)S(1)} %get-tuple-element.20), channel_id=1, source_target_pairs={{0,5},{1,4},{2,7},{3,6},{4,1},{5,0},{6,3},{7,2},{8,13},{9,12},{10,... | collective-permute-start | bytes 147464 | tf_op jit(solution)/shard_map/ppermute | solution.py:156
  10.4 6.9 %collective-permute-start.4 = (f32[96,128]{1,0:T(8,128)S(1)}, f32[96,128]{1,0:T(8,128)S(1)}, u32[]{:S(2)}, u32[]{:S(2)}) collective-permute-start(f32[96,128]{1,0:T(8,128)S(1)} %get-tuple-element.21), channel_id=1, source_target_pairs={{0,7},{1,6},{2,5},{3,4},{4,3},{5,2},{6,1},{7,0},{8,15},{9,14},{10,... | collective-permute-start | bytes 147464 | tf_op jit(solution)/shard_map/ppermute | solution.py:156
  12.7 4.6 %collective-permute-start.5 = (f32[96,128]{1,0:T(8,128)S(1)}, f32[96,128]{1,0:T(8,128)S(1)}, u32[]{:S(2)}, u32[]{:S(2)}) collective-permute-start(f32[96,128]{1,0:T(8,128)S(1)} %get-tuple-element.22), channel_id=1, source_target_pairs={{0,2},{1,3},{2,0},{3,1},{4,6},{5,7},{6,4},{7,5},{8,10},{9,11},{10,... | collective-permute-start | bytes 147464 | tf_op jit(solution)/shard_map/ppermute | solution.py:156
  13.1 4.6 %collective-permute-start.6 = (f32[96,128]{1,0:T(8,128)S(1)}, f32[96,128]{1,0:T(8,128)S(1)}, u32[]{:S(2)}, u32[]{:S(2)}) collective-permute-start(f32[96,128]{1,0:T(8,128)S(1)} %get-tuple-element.23), channel_id=1, source_target_pairs={{0,1},{1,0},{2,3},{3,2},{4,5},{5,4},{6,7},{7,6},{8,9},{9,8},{10,11... | collective-permute-start | bytes 147464 | tf_op jit(solution)/shard_map/ppermute | solution.py:156
  14.4 3.4 %copy-start.1 = (s32[192,1,4]{0,2,1:T(4,128)S(1)}, s32[192,1,4]{0,2,1:T(4,128)}, u32[]{:S(2)}) copy-start(s32[192,1,4]{0,2,1:T(4,128)} %param.6) | copy-start | bytes 9220
  14.4 3.4 %copy-start.2 = (s32[192]{0:T(256)S(1)}, s32[192]{0:T(256)}, u32[]{:S(2)}) copy-start(s32[192]{0:T(256)} %param.7) | copy-start | bytes 2308
  18.9 1.2 %collective-permute-start.7 = (f32[8,128]{1,0:T(8,128)S(1)}, f32[8,128]{1,0:T(8,128)S(1)}, u32[]{:S(2)}, u32[]{:S(2)}) collective-permute-start(f32[8,128]{1,0:T(8,128)S(1)} %get-tuple-element.27), channel_id=1, source_target_pairs={{0,8},{8,0},{16,24},{24,16},{1,9},{9,1},{17,25},{25,17},{2,10},{10... | collective-permute-start | bytes 12296 | tf_op jit(solution)/shard_map/ppermute | solution.py:180

commit v8 on v7

--- a/solution.py
+++ b/solution.py
@@ -72,10 +72,9 @@
 def project_kernel(partners, index_ref, *refs):
     count = len(partners)
     field_refs = refs[:count]
-    high_ref, low_ref, noise_ref, block_ref, out_ref, line_ref, weights = refs[count:]
+    high_ref, low_ref, noise_ref, block_ref, sums_ref, line_ref, weights = refs[count:]
     width = high_ref.shape[0] // (GROUPS * NCOLOR)
     rows = width // count
-    per = NEIG // count
     for partner, field_ref in zip(partners, field_refs):
         s = jnp.bitwise_xor(index_ref[0], partner)
         for color in range(NCOLOR):
@@ -103,13 +102,18 @@
     line_high, line_low = split(line)
     line_sum = lax.dot_general(onehot, line_high, dims, preferred_element_type=jnp.float32)
     line_sum += lax.dot_general(onehot, line_low, dims, preferred_element_type=jnp.float32)
-    sums = jnp.concatenate([real, imag], axis=0)
-    lines = jnp.concatenate([jnp.zeros((8, LINE_LANE), jnp.float32), line_sum], axis=1)
-    line_ref[...] = lines
+    sums_ref[...] = jnp.concatenate([real, imag], axis=0)
+    line_ref[...] = jnp.concatenate([jnp.zeros((8, LINE_LANE), jnp.float32), line_sum], axis=1)
+
+
+def spread_kernel(sums_ref, line_ref, out_ref):
+    count = out_ref.shape[0]
+    per = NEIG // count
+    sums = sums_ref[...]
     for j in range(count):
         pieces = [sums[8 * i : 8 * i + 8, per * j : per * (j + 1)] for i in range(COLS // 8)]
         pieces.append(jnp.zeros((8, 128 - per * len(pieces)), jnp.float32))
-        out_ref[j] = jnp.concatenate(pieces, axis=1) + lines
+        out_ref[j] = jnp.concatenate(pieces, axis=1) + line_ref[...]
 
 
 def join_kernel(part_ref, line_ref, out_ref):
@@ -168,16 +172,24 @@
         cost_estimate=pl.CostEstimate(flops=6 * eigvecs.size, bytes_accessed=8 * eigvecs.size, transcendentals=0),
         name="split",
     )(pltpu.with_memory_space_constraint(vectors, pltpu.HBM))
-    part, line = pl.pallas_call(
+    sums, line = pl.pallas_call(
         functools.partial(project_kernel, partners),
-        out_shape=(pltpu.VMEM((count, 8, 128), f32), pltpu.VMEM((8, 128), f32)),
+        out_shape=(pltpu.VMEM((COLS, NEIG), f32), pltpu.VMEM((8, 128), f32)),
         in_specs=[SMEM] + [VMEM] * (count + 4),
         out_specs=(VMEM, VMEM),
         scratch_shapes=[pltpu.VMEM((NCOLOR * sites // GROUPS, 128), f32)],
         compiler_params=pltpu.CompilerParams(vmem_limit_bytes=24 * 1024 * 1024),
         name="project",
     )(index, *received, high, low, jnp.transpose(sink_noise.reshape(NEIG, NSPIN)), eig_block.reshape(1, NEIG))
-    line = lax.ppermute(line, "tm", [(i, i ^ 1) for i in range(times)])
+    other_line = lax.ppermute(line, "tm", [(i, i ^ 1) for i in range(times)])
+    part = pl.pallas_call(
+        spread_kernel,
+        out_shape=pltpu.VMEM((count, 8, 128), f32),
+        in_specs=[VMEM, VMEM],
+        out_specs=VMEM,
+        compiler_params=pltpu.CompilerParams(vmem_limit_bytes=8 * 1024 * 1024),
+        name="spread",
+    )(sums, line)
     chips = times // CORES
     parts = pl.pallas_call(
         join_kernel,
@@ -186,7 +198,7 @@
         out_specs=VMEM,
         compiler_params=pltpu.CompilerParams(vmem_limit_bytes=8 * 1024 * 1024),
         name="join",
-    )(part, line)
+    )(part, other_line)
     groups = [
         [(chip * CORES + core) * count + s for chip in reversed(range(chips)) for s in reversed(range(count))]
         for core in range(CORES)

time: 30.8 us -> 30.8 us (level)
  transfers between devices with their start and end apart: 8 -> 8, of which waited for: 2 -> 2; matrix products, arithmetic and copies ran while one was open for 0% -> 0% of each run, Pallas kernels for 9% -> 10%
where the time goes in v8:
time: 30.8 us; the launch traced here: 30.6 us
  starting transfers between devices  12.5 us (41%)
  blocking collectives  9.71 us (32%)
  Pallas kernels  5.2 us (17%)
  waiting for transfers between devices  1.49 us (5%)
  local copies, waits for them, and re-layouts  1 us (3%)
  between operations  0.71 us (2%)
    ppermute x7, starting transfers between devices, body(): lax.ppermute(chunk, 'slab', [(i, i ^ partner) for i in range(count)])  12.5 us
    all_to_all x1, blocking collectives, body(): lax.all_to_all(parts.reshape(chips * count, 8, 128), ('tm', 'slab'), 0, 0...  9.71 us
    pallas_call x1, Pallas kernels, body(): pl.pallas_call(split_kernel, out_shape=(shape, shape), in_specs=[pl.Block...  2.88 us
    pallas_call x1, Pallas kernels, body(): pl.pallas_call(functools.partial(project_kernel, partners), out_shape=(pl...  1.2 us
    ppermute x1, waiting for transfers between devices, body(): other_line = lax.ppermute(line, 'tm', [(i, i ^ 1) for i in range(times)])  1.06 us
    unnamed x6, local copies, waits for them, and re-layouts  1 us
    pallas_call x1, Pallas kernels, body(): pl.pallas_call(functools.partial(finish_kernel, count, factor), out_shape...  0.74 us
  transfers between devices with their start and end apart: 8, of which 2 were waited for; matrix products, arithmetic and copies ran while one was open for 0% of the time, Pallas kernels for 10%

profile of v8, /device:TPU:0, one launch (start us, length us, event | category | flops | bytes accessed | tf_op | source)
XLA Modules:
  0.0 30.6 jit_solution(14703148883569843339)
XLA Ops:
  0.6 0.0 copy-start
  0.6 1.0 %copy-done = f32[1,96,1024]{2,1,0:T(8,128)S(1)} copy-done((f32[1,96,1024]{2,1,0:T(8,128)S(1)}, f32[1,96,1024]{2,1,0:T(8,128)}, u32[]{:S(2)}) %copy-start) | copy-done | bytes 393240
  1.6 0.3 pack.1
  1.9 4.1 %collective-permute-start = (f32[96,128]{1,0:T(8,128)S(1)}, f32[96,128]{1,0:T(8,128)S(1)}, u32[]{:S(2)}, u32[]{:S(2)}) collective-permute-start(f32[96,128]{1,0:T(8,128)S(1)} %get-tuple-element.17), channel_id=1, source_target_pairs={{0,4},{1,5},{2,6},{3,7},{4,0},{5,1},{6,2},{7,3},{8,12},{9,13},{10,... | collective-permute-start | bytes 147464 | tf_op jit(solution)/shard_map/ppermute | solution.py:160
  6.0 2.5 %collective-permute-start.1 = (f32[96,128]{1,0:T(8,128)S(1)}, f32[96,128]{1,0:T(8,128)S(1)}, u32[]{:S(2)}, u32[]{:S(2)}) collective-permute-start(f32[96,128]{1,0:T(8,128)S(1)} %get-tuple-element.18), channel_id=1, source_target_pairs={{0,3},{1,2},{2,1},{3,0},{4,7},{5,6},{6,5},{7,4},{8,11},{9,10},{10,... | collective-permute-start | bytes 147464 | tf_op jit(solution)/shard_map/ppermute | solution.py:160
  8.5 0.2 collective-permute-start.2
  8.7 1.7 %collective-permute-start.3 = (f32[96,128]{1,0:T(8,128)S(1)}, f32[96,128]{1,0:T(8,128)S(1)}, u32[]{:S(2)}, u32[]{:S(2)}) collective-permute-start(f32[96,128]{1,0:T(8,128)S(1)} %get-tuple-element.20), channel_id=1, source_target_pairs={{0,5},{1,4},{2,7},{3,6},{4,1},{5,0},{6,3},{7,2},{8,13},{9,12},{10,... | collective-permute-start | bytes 147464 | tf_op jit(solution)/shard_map/ppermute | solution.py:160
  10.4 2.3 %collective-permute-start.4 = (f32[96,128]{1,0:T(8,128)S(1)}, f32[96,128]{1,0:T(8,128)S(1)}, u32[]{:S(2)}, u32[]{:S(2)}) collective-permute-start(f32[96,128]{1,0:T(8,128)S(1)} %get-tuple-element.21), channel_id=1, source_target_pairs={{0,7},{1,6},{2,5},{3,4},{4,3},{5,2},{6,1},{7,0},{8,15},{9,14},{10,... | collective-permute-start | bytes 147464 | tf_op jit(solution)/shard_map/ppermute | solution.py:160
  12.7 0.0 collective-permute-done.refs_1_
  12.7 0.5 %collective-permute-start.5 = (f32[96,128]{1,0:T(8,128)S(1)}, f32[96,128]{1,0:T(8,128)S(1)}, u32[]{:S(2)}, u32[]{:S(2)}) collective-permute-start(f32[96,128]{1,0:T(8,128)S(1)} %get-tuple-element.22), channel_id=1, source_target_pairs={{0,2},{1,3},{2,0},{3,1},{4,6},{5,7},{6,4},{7,5},{8,10},{9,11},{10,... | collective-permute-start | bytes 147464 | tf_op jit(solution)/shard_map/ppermute | solution.py:160
  13.1 0.0 collective-permute-done.1.refs_2_
  13.1 1.2 %collective-permute-start.6 = (f32[96,128]{1,0:T(8,128)S(1)}, f32[96,128]{1,0:T(8,128)S(1)}, u32[]{:S(2)}, u32[]{:S(2)}) collective-permute-start(f32[96,128]{1,0:T(8,128)S(1)} %get-tuple-element.23), channel_id=1, source_target_pairs={{0,1},{1,0},{2,3},{3,2},{4,5},{5,4},{6,7},{7,6},{8,9},{9,8},{10,11... | collective-permute-start | bytes 147464 | tf_op jit(solution)/shard_map/ppermute | solution.py:160
  14.4 0.0 copy-start.1
  14.4 0.0 copy-start.2
  14.4 2.9 %split.1 = (bf16[3072,384]{1,0:T(8,128)(2,1)S(1)}, bf16[3072,384]{1,0:T(8,128)(2,1)S(1)}) custom-call(f32[2,3,192,1024]{3,2,1,0:T(8,128)} %bitcast.21), custom_call_target="tpu_custom_call" | custom-call | flops 7077888 | bytes 9437184 | tf_op jit(solution)/shard_map/split/pallas_call | solution.py:165
  17.3 0.0 collective-permute-done.2.refs_3_
  17.3 0.0 collective-permute-done.3.refs_4_
  17.3 0.0 collective-permute-done.4.refs_5_
  17.3 0.0 collective-permute-done.5.refs_6_
  17.3 0.4 %collective-permute-done.6.refs_7_ = f32[96,128]{1,0:T(8,128)S(1)} collective-permute-done((f32[96,128]{1,0:T(8,128)S(1)}, f32[96,128]{1,0:T(8,128)S(1)}, u32[]{:S(2)}, u32[]{:S(2)}) %collective-permute-start.6) | collective-permute-done | bytes 49184 | tf_op jit(solution)/shard_map/ppermute | solution.py:160
  17.7 0.0 copy-done.1
  17.7 0.0 copy-done.2
  17.7 1.2 %project.1 = (f32[32,192]{1,0:T(8,128)S(1)}, f32[8,128]{1,0:T(8,128)S(1)}) custom-call(s32[1]{0:T(128)} %bitcast.1.index_ref, f32[96,128]{1,0:T(8,128)S(1)} %get-tuple-element.16.refs_0_, f32[96,128]{1,0:T(8,128)S(1)} %collective-permute-done.refs_1_, f32[96,128]{1,0:T(8,128)S(1)} %collective-permute-done.1.refs_2_, ...), custom_call_target="tpu_custom_call" | custom-call | tf_op jit(solution)/shard_map/project/pallas_call | solution.py:175
  18.9 0.0 collective-permute-start.7
  18.9 0.1 spread.1.part_ref
  19.0 1.1 %collective-permute-done.7.line_ref = f32[8,128]{1,0:T(8,128)S(1)} collective-permute-done((f32[8,128]{1,0:T(8,128)S(1)}, f32[8,128]{1,0:T(8,128)S(1)}, u32[]{:S(2)}, u32[]{:S(2)}) %collective-permute-start.7) | collective-permute-done | bytes 4128 | tf_op jit(solution)/shard_map/ppermute | solution.py:184
  20.1 9.7 %all_to_all.5 = f32[16,8,128]{2,1,0:T(8,128)S(1)} all-to-all(f32[16,8,128]{2,1,0:T(8,128)S(1)} %bitcast.18), channel_id=1, replica_groups={{23,22,21,20,19,18,17,16,7,6,5,4,3,2,1,0},{31,30,29,28,27,26,25,24,15,1..., dimensions={0} | all-to-all | bytes 131072 | tf_op jit(solution)/shard_map/all_to_all | solution.py:206
  29.8 0.7 %finish.1 = (f32[32,24]{1,0:T(8,128)}, f32[2,4,8]{2,1,0:T(4,128)}) custom-call(s32[1]{0:T(128)} %bitcast.time_ref.index_ref, f32[2,8,8,128]{3,2,1,0:T(8,128)S(1)} %bitcast.17), custom_call_target="tpu_custom_call" | custom-call | tf_op jit(solution)/shard_map/finish/pallas_call | solution.py:210
  (1 shorter events, 0.0 us)
Async XLA Ops:
  0.6 1.0 %copy-start = (f32[1,96,1024]{2,1,0:T(8,128)S(1)}, f32[1,96,1024]{2,1,0:T(8,128)}, u32[]{:S(2)}) copy-start(f32[1,96,1024]{2,1,0:T(8,128)} %param.4) | copy-start | bytes 1179652
  1.9 10.8 %collective-permute-start = (f32[96,128]{1,0:T(8,128)S(1)}, f32[96,128]{1,0:T(8,128)S(1)}, u32[]{:S(2)}, u32[]{:S(2)}) collective-permute-start(f32[96,128]{1,0:T(8,128)S(1)} %get-tuple-element.17), channel_id=1, source_target_pairs={{0,4},{1,5},{2,6},{3,7},{4,0},{5,1},{6,2},{7,3},{8,12},{9,13},{10,... | collective-permute-start | bytes 147464 | tf_op jit(solution)/shard_map/ppermute | solution.py:160
  6.0 7.1 %collective-permute-start.1 = (f32[96,128]{1,0:T(8,128)S(1)}, f32[96,128]{1,0:T(8,128)S(1)}, u32[]{:S(2)}, u32[]{:S(2)}) collective-permute-start(f32[96,128]{1,0:T(8,128)S(1)} %get-tuple-element.18), channel_id=1, source_target_pairs={{0,3},{1,2},{2,1},{3,0},{4,7},{5,6},{6,5},{7,4},{8,11},{9,10},{10,... | collective-permute-start | bytes 147464 | tf_op jit(solution)/shard_map/ppermute | solution.py:160
  8.5 8.8 %collective-permute-start.2 = (f32[96,128]{1,0:T(8,128)S(1)}, f32[96,128]{1,0:T(8,128)S(1)}, u32[]{:S(2)}, u32[]{:S(2)}) collective-permute-start(f32[96,128]{1,0:T(8,128)S(1)} %get-tuple-element.19), channel_id=1, source_target_pairs={{0,6},{1,7},{2,4},{3,5},{4,2},{5,3},{6,0},{7,1},{8,14},{9,15},{10,... | collective-permute-start | bytes 147464 | tf_op jit(solution)/shard_map/ppermute | solution.py:160
  8.7 8.5 %collective-permute-start.3 = (f32[96,128]{1,0:T(8,128)S(1)}, f32[96,128]{1,0:T(8,128)S(1)}, u32[]{:S(2)}, u32[]{:S(2)}) collective-permute-start(f32[96,128]{1,0:T(8,128)S(1)} %get-tuple-element.20), channel_id=1, source_target_pairs={{0,5},{1,4},{2,7},{3,6},{4,1},{5,0},{6,3},{7,2},{8,13},{9,12},{10,... | collective-permute-start | bytes 147464 | tf_op jit(solution)/shard_map/ppermute | solution.py:160
  10.4 6.9 %collective-permute-start.4 = (f32[96,128]{1,0:T(8,128)S(1)}, f32[96,128]{1,0:T(8,128)S(1)}, u32[]{:S(2)}, u32[]{:S(2)}) collective-permute-start(f32[96,128]{1,0:T(8,128)S(1)} %get-tuple-element.21), channel_id=1, source_target_pairs={{0,7},{1,6},{2,5},{3,4},{4,3},{5,2},{6,1},{7,0},{8,15},{9,14},{10,... | collective-permute-start | bytes 147464 | tf_op jit(solution)/shard_map/ppermute | solution.py:160
  12.7 4.6 %collective-permute-start.5 = (f32[96,128]{1,0:T(8,128)S(1)}, f32[96,128]{1,0:T(8,128)S(1)}, u32[]{:S(2)}, u32[]{:S(2)}) collective-permute-start(f32[96,128]{1,0:T(8,128)S(1)} %get-tuple-element.22), channel_id=1, source_target_pairs={{0,2},{1,3},{2,0},{3,1},{4,6},{5,7},{6,4},{7,5},{8,10},{9,11},{10,... | collective-permute-start | bytes 147464 | tf_op jit(solution)/shard_map/ppermute | solution.py:160
  13.1 4.6 %collective-permute-start.6 = (f32[96,128]{1,0:T(8,128)S(1)}, f32[96,128]{1,0:T(8,128)S(1)}, u32[]{:S(2)}, u32[]{:S(2)}) collective-permute-start(f32[96,128]{1,0:T(8,128)S(1)} %get-tuple-element.23), channel_id=1, source_target_pairs={{0,1},{1,0},{2,3},{3,2},{4,5},{5,4},{6,7},{7,6},{8,9},{9,8},{10,11... | collective-permute-start | bytes 147464 | tf_op jit(solution)/shard_map/ppermute | solution.py:160
  14.4 3.4 %copy-start.1 = (s32[192,1,4]{0,2,1:T(4,128)S(1)}, s32[192,1,4]{0,2,1:T(4,128)}, u32[]{:S(2)}) copy-start(s32[192,1,4]{0,2,1:T(4,128)} %param.6) | copy-start | bytes 9220
  14.4 3.4 %copy-start.2 = (s32[192]{0:T(256)S(1)}, s32[192]{0:T(256)}, u32[]{:S(2)}) copy-start(s32[192]{0:T(256)} %param.7) | copy-start | bytes 2308
  18.9 1.2 %collective-permute-start.7 = (f32[8,128]{1,0:T(8,128)S(1)}, f32[8,128]{1,0:T(8,128)S(1)}, u32[]{:S(2)}, u32[]{:S(2)}) collective-permute-start(f32[8,128]{1,0:T(8,128)S(1)} %get-tuple-element.27.line_ref), channel_id=1, source_target_pairs={{0,8},{8,0},{16,24},{24,16},{1,9},{9,1},{17,25},{25,17},{2,10},{10... | collective-permute-start | bytes 12296 | tf_op jit(solution)/shard_map/ppermute | solution.py:184

commit v9 on v8

--- a/solution.py
+++ b/solution.py
@@ -16,6 +16,7 @@
 COLS = 2 * PAIRS
 GROUPS = 128 // COLS
 CORES = 2
+EARLY = 3
 LINE_LANE = 96
 
 ORDER = (4, 3, 6, 5, 7, 2, 1)
@@ -49,7 +50,16 @@
             out_ref[pl.ds(color * rows, rows), :] = turned[pl.ds(r, rows, stride=count), :]
 
 
-def split_kernel(vec_ref, high_ref, low_ref, landed, arrived):
+def place(count, partners, index_ref, field_refs, weights):
+    rows = weights.shape[0] // count
+    for partner, field_ref in zip(partners, field_refs):
+        s = jnp.bitwise_xor(index_ref[0], partner)
+        weights[pl.ds(s, rows, stride=count), :] = field_ref[...]
+
+
+def split_kernel(count, partners, index_ref, *refs):
+    field_refs = refs[: len(partners)]
+    vec_ref, high_ref, low_ref, weights, landed, arrived = refs[len(partners) :]
     width = vec_ref.shape[3] // GROUPS
     steps = [(part, color) for color in range(NCOLOR) for part in range(2)]
     copies = [
@@ -58,6 +68,7 @@
     ]
     for copy in copies:
         copy.start()
+    place(count, partners, index_ref, field_refs, weights)
     for color in range(NCOLOR):
         for copy in copies[2 * color : 2 * color + 2]:
             copy.wait()
@@ -69,16 +80,11 @@
             low_ref[rows, :] = low
 
 
-def project_kernel(partners, index_ref, *refs):
-    count = len(partners)
-    field_refs = refs[:count]
-    high_ref, low_ref, noise_ref, block_ref, sums_ref, line_ref, weights = refs[count:]
+def project_kernel(count, partners, index_ref, *refs):
+    field_refs = refs[: len(partners)]
+    _, high_ref, low_ref, noise_ref, block_ref, sums_ref, line_ref, weights = refs[len(partners) :]
     width = high_ref.shape[0] // (GROUPS * NCOLOR)
-    rows = width // count
-    for partner, field_ref in zip(partners, field_refs):
-        s = jnp.bitwise_xor(index_ref[0], partner)
-        for color in range(NCOLOR):
-            weights[pl.ds(color * width + s, rows, stride=count), :] = field_ref[pl.ds(color * rows, rows), :]
+    place(count, partners, index_ref, field_refs, weights)
     high, low = split(weights[...].T)
     dims = (((1,), (1,)), ((), ()))
     total = jnp.zeros((COLS, 2 * NEIG), jnp.float32)
@@ -162,25 +168,34 @@
     ]
     vectors = jnp.transpose(eigvecs.reshape(eigvecs.shape[1:]), (0, 2, 1, 3))
     shape = jax.ShapeDtypeStruct((NCOLOR * sites, 2 * NEIG), jnp.bfloat16)
-    high, low = pl.pallas_call(
-        split_kernel,
-        out_shape=(shape, shape),
-        in_specs=[pl.BlockSpec(memory_space=pltpu.HBM)],
-        out_specs=(VMEM, VMEM),
+    field = pltpu.VMEM((NCOLOR * sites // GROUPS, 128), f32)
+    high, low, placed = pl.pallas_call(
+        functools.partial(split_kernel, count, partners[:EARLY]),
+        out_shape=(shape, shape, field),
+        in_specs=[SMEM] + [VMEM] * EARLY + [pl.BlockSpec(memory_space=pltpu.HBM)],
+        out_specs=(VMEM, VMEM, VMEM),
         scratch_shapes=[pltpu.VMEM(vectors.shape, f32), pltpu.SemaphoreType.DMA((2 * NCOLOR,))],
         compiler_params=pltpu.CompilerParams(vmem_limit_bytes=24 * 1024 * 1024),
         cost_estimate=pl.CostEstimate(flops=6 * eigvecs.size, bytes_accessed=8 * eigvecs.size, transcendentals=0),
         name="split",
-    )(pltpu.with_memory_space_constraint(vectors, pltpu.HBM))
-    sums, line = pl.pallas_call(
-        functools.partial(project_kernel, partners),
-        out_shape=(pltpu.VMEM((COLS, NEIG), f32), pltpu.VMEM((8, 128), f32)),
-        in_specs=[SMEM] + [VMEM] * (count + 4),
-        out_specs=(VMEM, VMEM),
-        scratch_shapes=[pltpu.VMEM((NCOLOR * sites // GROUPS, 128), f32)],
+    )(index, *received[:EARLY], pltpu.with_memory_space_constraint(vectors, pltpu.HBM))
+    sums, line, _ = pl.pallas_call(
+        functools.partial(project_kernel, count, partners[EARLY:]),
+        out_shape=(pltpu.VMEM((COLS, NEIG), f32), pltpu.VMEM((8, 128), f32), field),
+        in_specs=[SMEM] + [VMEM] * (count - EARLY + 5),
+        out_specs=(VMEM, VMEM, VMEM),
+        input_output_aliases={count - EARLY + 1: 2},
         compiler_params=pltpu.CompilerParams(vmem_limit_bytes=24 * 1024 * 1024),
         name="project",
-    )(index, *received, high, low, jnp.transpose(sink_noise.reshape(NEIG, NSPIN)), eig_block.reshape(1, NEIG))
+    )(
+        index,
+        *received[EARLY:],
+        placed,
+        high,
+        low,
+        jnp.transpose(sink_noise.reshape(NEIG, NSPIN)),
+        eig_block.reshape(1, NEIG),
+    )
     other_line = lax.ppermute(line, "tm", [(i, i ^ 1) for i in range(times)])
     part = pl.pallas_call(
         spread_kernel,

time: 30.8 us -> 30.7 us (level)
  no operation moved by 1% of the time
where the time goes in v9:
time: 30.7 us; the launch traced here: 30.5 us
  starting transfers between devices  12.5 us (41%)
  blocking collectives  9.71 us (32%)
  Pallas kernels  5.17 us (17%)
  waiting for transfers between devices  1.49 us (5%)
  local copies, waits for them, and re-layouts  1 us (3%)
  between operations  0.71 us (2%)
    ppermute x7, starting transfers between devices, body(): lax.ppermute(chunk, 'slab', [(i, i ^ partner) for i in range(count)])  12.5 us
    all_to_all x1, blocking collectives, body(): lax.all_to_all(parts.reshape(chips * count, 8, 128), ('tm', 'slab'), 0, 0...  9.71 us
    pallas_call x1, Pallas kernels, body(): pl.pallas_call(functools.partial(split_kernel, count, partners[:EARLY]),...  2.88 us
    pallas_call x1, Pallas kernels, body(): pl.pallas_call(functools.partial(project_kernel, count, partners[EARLY:])...  1.18 us
    ppermute x1, waiting for transfers between devices, body(): other_line = lax.ppermute(line, 'tm', [(i, i ^ 1) for i in range(times)])  1.06 us
    unnamed x6, local copies, waits for them, and re-layouts  1 us
    pallas_call x1, Pallas kernels, body(): pl.pallas_call(functools.partial(finish_kernel, count, factor), out_shape...  0.74 us
  transfers between devices with their start and end apart: 8, of which 2 were waited for; matrix products, arithmetic and copies ran while one was open for 0% of the time, Pallas kernels for 10%

profile of v9, /device:TPU:0, one launch (start us, length us, event | category | flops | bytes accessed | tf_op | source)
XLA Modules:
  0.0 30.5 jit_solution(17253733187454887783)
XLA Ops:
  0.6 0.0 copy-start
  0.6 1.0 %copy-done = f32[1,96,1024]{2,1,0:T(8,128)S(1)} copy-done((f32[1,96,1024]{2,1,0:T(8,128)S(1)}, f32[1,96,1024]{2,1,0:T(8,128)}, u32[]{:S(2)}) %copy-start) | copy-done | bytes 393240
  1.6 0.3 pack.1
  1.9 4.1 %collective-permute-start.5 = (f32[96,128]{1,0:T(8,128)S(1)}, f32[96,128]{1,0:T(8,128)S(1)}, u32[]{:S(2)}, u32[]{:S(2)}) collective-permute-start(f32[96,128]{1,0:T(8,128)S(1)} %get-tuple-element.23), channel_id=1, source_target_pairs={{0,4},{1,5},{2,6},{3,7},{4,0},{5,1},{6,2},{7,3},{8,12},{9,13},{10,... | collective-permute-start | bytes 147464 | tf_op jit(solution)/shard_map/ppermute | solution.py:166
  6.0 2.5 %collective-permute-start.6 = (f32[96,128]{1,0:T(8,128)S(1)}, f32[96,128]{1,0:T(8,128)S(1)}, u32[]{:S(2)}, u32[]{:S(2)}) collective-permute-start(f32[96,128]{1,0:T(8,128)S(1)} %get-tuple-element.24), channel_id=1, source_target_pairs={{0,3},{1,2},{2,1},{3,0},{4,7},{5,6},{6,5},{7,4},{8,11},{9,10},{10,... | collective-permute-start | bytes 147464 | tf_op jit(solution)/shard_map/ppermute | solution.py:166
  8.5 0.2 collective-permute-start
  8.7 1.7 %collective-permute-start.1 = (f32[96,128]{1,0:T(8,128)S(1)}, f32[96,128]{1,0:T(8,128)S(1)}, u32[]{:S(2)}, u32[]{:S(2)}) collective-permute-start(f32[96,128]{1,0:T(8,128)S(1)} %get-tuple-element.18), channel_id=1, source_target_pairs={{0,5},{1,4},{2,7},{3,6},{4,1},{5,0},{6,3},{7,2},{8,13},{9,12},{10,... | collective-permute-start | bytes 147464 | tf_op jit(solution)/shard_map/ppermute | solution.py:166
  10.4 2.3 %collective-permute-start.2 = (f32[96,128]{1,0:T(8,128)S(1)}, f32[96,128]{1,0:T(8,128)S(1)}, u32[]{:S(2)}, u32[]{:S(2)}) collective-permute-start(f32[96,128]{1,0:T(8,128)S(1)} %get-tuple-element.19), channel_id=1, source_target_pairs={{0,7},{1,6},{2,5},{3,4},{4,3},{5,2},{6,1},{7,0},{8,15},{9,14},{10,... | collective-permute-start | bytes 147464 | tf_op jit(solution)/shard_map/ppermute | solution.py:166
  12.7 0.0 collective-permute-done.5.refs_1_
  12.7 0.5 %collective-permute-start.3 = (f32[96,128]{1,0:T(8,128)S(1)}, f32[96,128]{1,0:T(8,128)S(1)}, u32[]{:S(2)}, u32[]{:S(2)}) collective-permute-start(f32[96,128]{1,0:T(8,128)S(1)} %get-tuple-element.20), channel_id=1, source_target_pairs={{0,2},{1,3},{2,0},{3,1},{4,6},{5,7},{6,4},{7,5},{8,10},{9,11},{10,... | collective-permute-start | bytes 147464 | tf_op jit(solution)/shard_map/ppermute | solution.py:166
  13.1 0.0 collective-permute-done.6.refs_2_
  13.1 1.2 %collective-permute-start.4 = (f32[96,128]{1,0:T(8,128)S(1)}, f32[96,128]{1,0:T(8,128)S(1)}, u32[]{:S(2)}, u32[]{:S(2)}) collective-permute-start(f32[96,128]{1,0:T(8,128)S(1)} %get-tuple-element.21), channel_id=1, source_target_pairs={{0,1},{1,0},{2,3},{3,2},{4,5},{5,4},{6,7},{7,6},{8,9},{9,8},{10,11... | collective-permute-start | bytes 147464 | tf_op jit(solution)/shard_map/ppermute | solution.py:166
  14.4 0.0 copy-start.1
  14.4 0.0 copy-start.2
  14.4 2.9 %split.1 = (bf16[3072,384]{1,0:T(8,128)(2,1)S(1)}, bf16[3072,384]{1,0:T(8,128)(2,1)S(1)}, f32[768,128]{1,0:T(8,128)S(1)}) custom-call(s32[1]{0:T(128)} %bitcast.1.index_ref, f32[96,128]{1,0:T(8,128)S(1)} %get-tuple-element.22.refs_0_, f32[96,128]{1,0:T(8,128)S(1)} %collective-permute-done.5.refs_1_, f32[96,128]{1,0:T(8,128)S(1)} %collective-permute-done.6.refs_2_, ...), custom_call_target="tpu_custom_call" | custom-call | flops 7077888 | bytes 9437184 | tf_op jit(solution)/shard_map/split/pallas_call | solution.py:172
  17.3 0.0 collective-permute-done.refs_0_
  17.3 0.0 collective-permute-done.1.refs_1_
  17.3 0.0 collective-permute-done.2.refs_2_
  17.3 0.0 collective-permute-done.3.refs_3_
  17.3 0.4 %collective-permute-done.4.refs_4_ = f32[96,128]{1,0:T(8,128)S(1)} collective-permute-done((f32[96,128]{1,0:T(8,128)S(1)}, f32[96,128]{1,0:T(8,128)S(1)}, u32[]{:S(2)}, u32[]{:S(2)}) %collective-permute-start.4) | collective-permute-done | bytes 49184 | tf_op jit(solution)/shard_map/ppermute | solution.py:166
  17.7 0.0 copy-done.1
  17.7 0.0 copy-done.2
  17.7 1.2 %project.1 = (f32[32,192]{1,0:T(8,128)S(1)}, f32[8,128]{1,0:T(8,128)S(1)}, f32[768,128]{1,0:T(8,128)S(1)}) custom-call(s32[1]{0:T(128)} %bitcast.1.index_ref, f32[96,128]{1,0:T(8,128)S(1)} %collective-permute-done.refs_0_, f32[96,128]{1,0:T(8,128)S(1)} %collective-permute-done.1.refs_1_, ...), custom_call_target="tpu_custom_call", output_to_operand_aliasing={{2}: (6, {})} | custom-call | tf_op jit(solution)/shard_map/project/pallas_call | solution.py:182
  18.9 0.0 collective-permute-start.7
  18.9 0.1 spread.1.part_ref
  19.0 1.1 %collective-permute-done.7.line_ref = f32[8,128]{1,0:T(8,128)S(1)} collective-permute-done((f32[8,128]{1,0:T(8,128)S(1)}, f32[8,128]{1,0:T(8,128)S(1)}, u32[]{:S(2)}, u32[]{:S(2)}) %collective-permute-start.7) | collective-permute-done | bytes 4128 | tf_op jit(solution)/shard_map/ppermute | solution.py:199
  20.1 9.7 %all_to_all.5 = f32[16,8,128]{2,1,0:T(8,128)S(1)} all-to-all(f32[16,8,128]{2,1,0:T(8,128)S(1)} %bitcast.18), channel_id=1, replica_groups={{23,22,21,20,19,18,17,16,7,6,5,4,3,2,1,0},{31,30,29,28,27,26,25,24,15,1..., dimensions={0} | all-to-all | bytes 131072 | tf_op jit(solution)/shard_map/all_to_all | solution.py:221
  29.8 0.7 %finish.1 = (f32[32,24]{1,0:T(8,128)}, f32[2,4,8]{2,1,0:T(4,128)}) custom-call(s32[1]{0:T(128)} %bitcast.time_ref.index_ref, f32[2,8,8,128]{3,2,1,0:T(8,128)S(1)} %bitcast.17), custom_call_target="tpu_custom_call" | custom-call | tf_op jit(solution)/shard_map/finish/pallas_call | solution.py:225
  (1 shorter events, 0.0 us)
Async XLA Ops:
  0.6 1.0 %copy-start = (f32[1,96,1024]{2,1,0:T(8,128)S(1)}, f32[1,96,1024]{2,1,0:T(8,128)}, u32[]{:S(2)}) copy-start(f32[1,96,1024]{2,1,0:T(8,128)} %param.4) | copy-start | bytes 1179652
  1.9 10.8 %collective-permute-start.5 = (f32[96,128]{1,0:T(8,128)S(1)}, f32[96,128]{1,0:T(8,128)S(1)}, u32[]{:S(2)}, u32[]{:S(2)}) collective-permute-start(f32[96,128]{1,0:T(8,128)S(1)} %get-tuple-element.23), channel_id=1, source_target_pairs={{0,4},{1,5},{2,6},{3,7},{4,0},{5,1},{6,2},{7,3},{8,12},{9,13},{10,... | collective-permute-start | bytes 147464 | tf_op jit(solution)/shard_map/ppermute | solution.py:166
  6.0 7.1 %collective-permute-start.6 = (f32[96,128]{1,0:T(8,128)S(1)}, f32[96,128]{1,0:T(8,128)S(1)}, u32[]{:S(2)}, u32[]{:S(2)}) collective-permute-start(f32[96,128]{1,0:T(8,128)S(1)} %get-tuple-element.24), channel_id=1, source_target_pairs={{0,3},{1,2},{2,1},{3,0},{4,7},{5,6},{6,5},{7,4},{8,11},{9,10},{10,... | collective-permute-start | bytes 147464 | tf_op jit(solution)/shard_map/ppermute | solution.py:166
  8.5 8.8 %collective-permute-start = (f32[96,128]{1,0:T(8,128)S(1)}, f32[96,128]{1,0:T(8,128)S(1)}, u32[]{:S(2)}, u32[]{:S(2)}) collective-permute-start(f32[96,128]{1,0:T(8,128)S(1)} %get-tuple-element.17), channel_id=1, source_target_pairs={{0,6},{1,7},{2,4},{3,5},{4,2},{5,3},{6,0},{7,1},{8,14},{9,15},{10,... | collective-permute-start | bytes 147464 | tf_op jit(solution)/shard_map/ppermute | solution.py:166
  8.7 8.5 %collective-permute-start.1 = (f32[96,128]{1,0:T(8,128)S(1)}, f32[96,128]{1,0:T(8,128)S(1)}, u32[]{:S(2)}, u32[]{:S(2)}) collective-permute-start(f32[96,128]{1,0:T(8,128)S(1)} %get-tuple-element.18), channel_id=1, source_target_pairs={{0,5},{1,4},{2,7},{3,6},{4,1},{5,0},{6,3},{7,2},{8,13},{9,12},{10,... | collective-permute-start | bytes 147464 | tf_op jit(solution)/shard_map/ppermute | solution.py:166
  10.4 6.9 %collective-permute-start.2 = (f32[96,128]{1,0:T(8,128)S(1)}, f32[96,128]{1,0:T(8,128)S(1)}, u32[]{:S(2)}, u32[]{:S(2)}) collective-permute-start(f32[96,128]{1,0:T(8,128)S(1)} %get-tuple-element.19), channel_id=1, source_target_pairs={{0,7},{1,6},{2,5},{3,4},{4,3},{5,2},{6,1},{7,0},{8,15},{9,14},{10,... | collective-permute-start | bytes 147464 | tf_op jit(solution)/shard_map/ppermute | solution.py:166
  12.7 4.6 %collective-permute-start.3 = (f32[96,128]{1,0:T(8,128)S(1)}, f32[96,128]{1,0:T(8,128)S(1)}, u32[]{:S(2)}, u32[]{:S(2)}) collective-permute-start(f32[96,128]{1,0:T(8,128)S(1)} %get-tuple-element.20), channel_id=1, source_target_pairs={{0,2},{1,3},{2,0},{3,1},{4,6},{5,7},{6,4},{7,5},{8,10},{9,11},{10,... | collective-permute-start | bytes 147464 | tf_op jit(solution)/shard_map/ppermute | solution.py:166
  13.1 4.6 %collective-permute-start.4 = (f32[96,128]{1,0:T(8,128)S(1)}, f32[96,128]{1,0:T(8,128)S(1)}, u32[]{:S(2)}, u32[]{:S(2)}) collective-permute-start(f32[96,128]{1,0:T(8,128)S(1)} %get-tuple-element.21), channel_id=1, source_target_pairs={{0,1},{1,0},{2,3},{3,2},{4,5},{5,4},{6,7},{7,6},{8,9},{9,8},{10,11... | collective-permute-start | bytes 147464 | tf_op jit(solution)/shard_map/ppermute | solution.py:166
  14.4 3.4 %copy-start.1 = (s32[192,1,4]{0,2,1:T(4,128)S(1)}, s32[192,1,4]{0,2,1:T(4,128)}, u32[]{:S(2)}) copy-start(s32[192,1,4]{0,2,1:T(4,128)} %param.6) | copy-start | bytes 9220
  14.4 3.4 %copy-start.2 = (s32[192]{0:T(256)S(1)}, s32[192]{0:T(256)}, u32[]{:S(2)}) copy-start(s32[192]{0:T(256)} %param.7) | copy-start | bytes 2308
  18.9 1.2 %collective-permute-start.7 = (f32[8,128]{1,0:T(8,128)S(1)}, f32[8,128]{1,0:T(8,128)S(1)}, u32[]{:S(2)}, u32[]{:S(2)}) collective-permute-start(f32[8,128]{1,0:T(8,128)S(1)} %get-tuple-element.29.line_ref), channel_id=1, source_target_pairs={{0,8},{8,0},{16,24},{24,16},{1,9},{9,1},{17,25},{25,17},{2,10},{10... | collective-permute-start | bytes 12296 | tf_op jit(solution)/shard_map/ppermute | solution.py:199
